TPU v7x, 128 devices: a whole 4x4x4 slice. The times are simulated.
128 devices in a mesh: grp: 4 (over y_lo, core), col: 32 (over y_hi, x, z).
Axes of the slice: x: 4, y: 4 (y_hi: 2, y_lo: 2; y = y_hi * 2 + y_lo), z: 4, core: 2. Of those that a mesh axis runs over, the one named last changes fastest.
Arguments:
- interferogram: float32 [512, 512, 2048], P('grp', 'col'), may hold values from -6 to 6
- sideband_start: int32 [1], replicated, may hold values from 1 to 767
- crop_start: int32 [2], replicated, may hold values from 0 to 384
Outputs:
- focal_field: float32 [2, 256, 128, 128], P(None, ('grp', 'col'))
All inputs are finite; a program needn't handle non-finite values.
Results may differ from a plain program's by a relative error of at most 0.00007.
Values sent between devices are 32-bit elements; how exact they have to be, the bound alone decides.
No kernel may reach another device: no remote copies, remote signals or barrier semaphores. Data moves between devices by JAX's collectives and lax.ppermute only.
A program may use at most 128 MiB of HBM per device.

v0:
```python
import functools
import math

import jax
import jax.numpy as jnp
from jax import lax
from jax.experimental import pallas as pl
from jax.experimental.pallas import tpu as pltpu
from jax.sharding import PartitionSpec as P

NR = 512
NC = 512
NT = 2048
NB = 256
CROP = 128
HALF = NT // 2
TURN = 2048
F32 = jnp.float32
BF16 = jnp.bfloat16


def cos_sin(u):
    v = u + 256
    quadrant = (v >> 9) & 3
    r = ((v & 511) - 256).astype(F32) * (2.0 * math.pi / TURN)
    z = r * r
    s = r + r * z * (-1.6666654611e-1 + z * (8.3321608736e-3 + z * -1.9515295891e-4))
    c = 1.0 - 0.5 * z + z * z * (4.166664568298827e-2 + z * (-1.388731625493765e-3 + z * 2.443315711809948e-5))
    odd = (quadrant & 1) == 1
    cos = jnp.where(odd, s, c)
    sin = jnp.where(odd, c, s)
    cos = jnp.where((quadrant == 1) | (quadrant == 2), -cos, cos)
    sin = jnp.where(quadrant >= 2, -sin, sin)
    return cos, sin


def split(a):
    hi = a.astype(BF16)
    return hi, (a - hi.astype(F32)).astype(BF16)


def dot(a, b, dims):
    return lax.dot_general(a, b, (dims, ((), ())), preferred_element_type=F32)


def dot3(a, b, dims):
    return dot(a[0], b[0], dims) + (dot(a[0], b[1], dims) + dot(a[1], b[0], dims))


NT_DIMS = ((1,), (1,))
NN_DIMS = ((1,), (0,))
TN_DIMS = ((0,), (0,))


def spectrum_kernel(scal, x_hbm, send_ref, keep_ref, xbuf, tab_hi, tab_lo, row_hi, row_lo, sums, sem):
    start, crop, core, row0 = scal[0], scal[1], scal[2], scal[3]
    copies = []
    for h in range(2):
        for tt in range(16):
            cp = pltpu.make_async_copy(
                x_hbm.at[:, pl.ds(8 * h, 8), pl.ds(128 * tt, 128)], xbuf.at[h, tt], sem.at[h, tt]
            )
            cp.start()
            copies.append(cp)

    scale = 1.0 / math.sqrt(NT)

    def one_table(i, _):
        e = i >> 3
        m = (i & 7) * 16 + lax.broadcasted_iota(jnp.int32, (16, HALF), 0)
        t = lax.broadcasted_iota(jnp.int32, (16, HALF), 1)
        owner = jnp.where(m < 64, 1 - core, core)
        j = (m & 32) * 2 + owner * 32 + (m & 31)
        cos, sin = cos_sin(((start + 2 * j + e) * t) & (TURN - 1))
        for part, val in ((0, cos * scale), (1, sin * -scale)):
            hi, lo = split(val)
            rows = pl.ds(pl.multiple_of(e * 256 + part * 128 + (i & 7) * 16, 16), 16)
            tab_hi[rows, :] = hi
            tab_lo[rows, :] = lo
        return 0

    lax.fori_loop(0, 16, one_table, 0)

    rscale = 1.0 / math.sqrt(NR)
    r = row0 + lax.broadcasted_iota(jnp.int32, (128, CROP), 0)
    p = crop + lax.broadcasted_iota(jnp.int32, (128, CROP), 1)
    cos, sin = cos_sin(((r * p) & (NR - 1)) * (TURN // NR))
    cos, sin = cos * rscale, sin * rscale
    for rows, cols, val in ((0, 0, cos), (0, 128, -sin), (128, 0, sin), (128, 128, cos)):
        hi, lo = split(val)
        row_hi[rows : rows + 128, cols : cols + 128] = hi
        row_lo[rows : rows + 128, cols : cols + 128] = lo

    sign = jnp.where((start & 1) == 0, 1.0, -1.0).astype(F32)

    for h in range(2):
        for tt in range(16):
            copies[16 * h + tt].wait()
        xr = xbuf.at[h].reshape(16, 1024, 128)

        def pair(i, _):
            parts = [[], []]
            for cc in range(2):
                rows = pl.ds(2 * i + cc, 128, stride=8)
                a = [xr[tt, rows, :] for tt in range(8)]
                b = [xr[8 + tt, rows, :] * sign for tt in range(8)]
                parts[0].append(jnp.concatenate([v + w for v, w in zip(a, b)], axis=1))
                parts[1].append(jnp.concatenate([v - w for v, w in zip(a, b)], axis=1))
            for e in range(2):
                y = split(jnp.concatenate(parts[e], axis=0))
                d = dot3(
                    (tab_hi[256 * e : 256 * e + 256, :], tab_lo[256 * e : 256 * e + 256, :]), y, NT_DIMS
                )
                for cc in range(2):
                    rows = pl.ds(pl.multiple_of((e * 8 + 2 * i + cc) * 128, 128), 128)
                    sums[rows, 0:128] = d[0:128, 128 * cc : 128 * cc + 128]
                    sums[rows, 128:256] = d[128:256, 128 * cc : 128 * cc + 128]
            return 0

        lax.fori_loop(0, 4, pair, 0)

        def rowwise(i, _):
            rows = pl.ds(pl.multiple_of(i * 512, 512), 512)
            g = dot3(split(sums[rows, :]), (row_hi[...], row_lo[...]), NN_DIMS)
            for k in range(4):
                ec = i * 4 + k
                first = (ec // 8) * 32 + 8 * h + ec % 8
                for rel, ref in ((0, send_ref), (1, keep_ref)):
                    for y in range(2):
                        at = k * 128 + rel * 64 + y * 32
                        for ri in range(2):
                            ref[pl.ds(y * 64 + ri * 16 + first, 32, stride=128), :] = g[
                                at : at + 32, 128 * ri : 128 * ri + 128
                            ]
            return 0

        lax.fori_loop(0, 4, rowwise, 0)


def spectrum_call(scal, x):
    out = jax.ShapeDtypeStruct((4096, 128), F32)
    return pl.pallas_call(
        spectrum_kernel,
        out_shape=(out, out),
        in_specs=[pl.BlockSpec(memory_space=pltpu.SMEM), pl.BlockSpec(memory_space=pl.ANY)],
        out_specs=(pl.BlockSpec(memory_space=pltpu.VMEM), pl.BlockSpec(memory_space=pltpu.VMEM)),
        scratch_shapes=[
            pltpu.VMEM((2, 16, 128, 8, 128), F32),
            pltpu.VMEM((512, HALF), BF16),
            pltpu.VMEM((512, HALF), BF16),
            pltpu.VMEM((256, 256), BF16),
            pltpu.VMEM((256, 256), BF16),
            pltpu.VMEM((2048, 256), F32),
            pltpu.SemaphoreType.DMA((2, 16)),
        ],
        compiler_params=pltpu.CompilerParams(vmem_limit_bytes=48 * 2**20),
        name="spectrum",
    )(scal, x)


def focal_kernel(scal, g_ref, send_ref, keep_ref, tab_hi, tab_lo):
    crop, mine = scal[0], scal[1]
    scale = 1.0 / math.sqrt(NC)
    c = lax.broadcasted_iota(jnp.int32, (NC, CROP), 0)
    q = crop + lax.broadcasted_iota(jnp.int32, (NC, CROP), 1)
    cos, sin = cos_sin(((c * q) & (NC - 1)) * (TURN // NC))
    for lane, val in ((0, cos * scale), (128, sin * scale)):
        hi, lo = split(val)
        tab_hi[:, lane : lane + 128] = hi
        tab_lo[:, lane : lane + 128] = lo
    for rel, ref in ((0, send_ref), (1, keep_ref)):
        y = 1 - mine if rel == 0 else mine
        for e in range(2):
            g = [g_ref[:, y, e, ri, :, :].reshape(NC, CROP) for ri in range(2)]
            g = jnp.concatenate(g, axis=1)
            u = dot3(split(g), (tab_hi[...], tab_lo[...]), TN_DIMS)
            ref[0, e] = u[0:128, 0:128] + u[128:256, 128:256]
            ref[1, e] = u[128:256, 0:128] - u[0:128, 128:256]


def focal_call(scal, g):
    out = jax.ShapeDtypeStruct((2, 2, CROP, CROP), F32)
    return pl.pallas_call(
        focal_kernel,
        out_shape=(out, out),
        in_specs=[pl.BlockSpec(memory_space=pltpu.SMEM), pl.BlockSpec(memory_space=pltpu.VMEM)],
        out_specs=(pl.BlockSpec(memory_space=pltpu.VMEM), pl.BlockSpec(memory_space=pltpu.VMEM)),
        scratch_shapes=[pltpu.VMEM((NC, 256), BF16), pltpu.VMEM((NC, 256), BF16)],
        compiler_params=pltpu.CompilerParams(vmem_limit_bytes=24 * 2**20),
        name="focal",
    )(scal, g)


def on_device(interferogram, sideband_start, crop_start):
    grp = lax.axis_index("grp")
    core, y_lo = grp & 1, grp >> 1
    scal = jnp.stack([sideband_start[0], crop_start[0], core, grp * 128]).astype(jnp.int32)
    send, keep = spectrum_call(scal, interferogram)
    got = lax.ppermute(send, "grp", [(i, i ^ 1) for i in range(4)])
    mine = (keep + got).reshape(32, 128, 128)
    gathered = lax.all_to_all(mine, "col", split_axis=0, concat_axis=0, tiled=True)
    scal = jnp.stack([crop_start[1], y_lo]).astype(jnp.int32)
    send, keep = focal_call(scal, gathered.reshape(32, 2, 2, 2, 16, 128))
    got = lax.ppermute(send, "grp", [(i, i ^ 2) for i in range(4)])
    return keep + got


def solution(mesh):
    return jax.shard_map(
        on_device,
        mesh=mesh,
        in_specs=(P("grp", "col", None), P(), P()),
        out_specs=P(None, ("grp", "col"), None, None),
        check_vma=False,
    )
```

profile of v0, /device:TPU:0, one launch (start us, length us, event | category | flops | bytes accessed | tf_op | source)
XLA Modules:
  0.0 80.4 jit_solution(14127906022075470010)
XLA Ops:
  0.7 1.4 %fusion = (s32[1]{0:T(128)}, s32[1]{0:T(128)}) fusion(s32[2]{0:T(128)} %param.5), kind=kLoop, calls=%fused_computation.2 | loop fusion | bytes 16 | tf_op jit(solution)/shard_map/slice | solution.py:197
  2.0 0.7 pad_add_fusion.1.scal
  2.8 20.8 %spectrum.1 = (f32[4096,128]{1,0:T(8,128)S(1)}, f32[4096,128]{1,0:T(8,128)S(1)}) custom-call(s32[4]{0:T(128)S(1)} %pad_add_fusion.1.scal, f32[128,16,2048]{2,1,0:T(8,128)} %x_hbm.1), custom_call_target="tpu_custom_call" | custom-call | tf_op jit(solution)/shard_map/spectrum/pallas_call | solution.py:142
  23.5 0.1 collective-permute-start
  23.6 4.1 %collective-permute-done = f32[4096,128]{1,0:T(8,128)S(1)} collective-permute-done((f32[4096,128]{1,0:T(8,128)S(1)}, f32[4096,128]{1,0:T(8,128)S(1)}, u32[]{:S(2)}, u32[]{:S(2)}) %collective-permute-start) | collective-permute-done | bytes 2097184 | tf_op jit(solution)/shard_map/ppermute | solution.py:199
  27.8 1.6 %add.6 = f32[4096,128]{1,0:T(8,128)} add(f32[4096,128]{1,0:T(8,128)S(1)} %get-tuple-element.9, f32[4096,128]{1,0:T(8,128)S(1)} %collective-permute-done) | non-fusion elementwise | flops 524288 | bytes 6291456 | tf_op jit(solution)/shard_map/add | solution.py:200
  29.4 10.9 %all-to-all-start = ((f32[32,128,128]{2,1,0:T(8,128)}), f32[32,128,128]{2,1,0:T(8,128)S(1)}, u32[]{:S(2)}, u32[]{:S(2)}) async-start(f32[32,128,128]{2,1,0:T(8,128)} %bitcast.6), calls=%async_computation | async-start | bytes 4194304 | tf_op jit(solution)/shard_map/all_to_all | solution.py:201
  40.3 0.8 pad_add_fusion.scal
  41.0 29.2 %all-to-all-done = f32[32,128,128]{2,1,0:T(8,128)S(1)} async-done(((f32[32,128,128]{2,1,0:T(8,128)}), f32[32,128,128]{2,1,0:T(8,128)S(1)}, u32[]{:S(2)}, u32[]{:S(2)}) %all-to-all-start) | async-done | bytes 2097184 | tf_op jit(solution)/shard_map/all_to_all | solution.py:201
  70.3 2.0 %focal.1 = (f32[2,2,128,128]{3,2,1,0:T(8,128)S(1)}, f32[2,2,128,128]{3,2,1,0:T(8,128)S(1)}) custom-call(s32[2]{0:T(128)S(1)} %pad_add_fusion.scal, f32[32,2,2,2,16,128]{5,4,3,2,1,0:T(8,128)S(1)} %bitcast.5), custom_call_target="tpu_custom_call" | custom-call | tf_op jit(solution)/shard_map/focal/pallas_call | solution.py:183
  72.3 2.5 %collective-permute-start.1 = (f32[2,2,128,128]{3,2,1,0:T(8,128)S(1)}, f32[2,2,128,128]{3,2,1,0:T(8,128)S(1)}, u32[]{:S(2)}, u32[]{:S(2)}) collective-permute-start(f32[2,2,128,128]{3,2,1,0:T(8,128)S(1)} %get-tuple-element.12), channel_id=1, source_target_pairs={{0,64},{32,96},{64,0},{96,32},{1,65},{33,97},{65,1},{97,33},{2,66}... | collective-permute-start | bytes 786440 | tf_op jit(solution)/shard_map/ppermute | solution.py:204
  74.8 4.9 %collective-permute-done.1 = f32[2,2,128,128]{3,2,1,0:T(8,128)S(1)} collective-permute-done((f32[2,2,128,128]{3,2,1,0:T(8,128)S(1)}, f32[2,2,128,128]{3,2,1,0:T(8,128)S(1)}, u32[]{:S(2)}, u32[]{:S(2)}) %collective-permute-start.1) | collective-permute-done | bytes 262176 | tf_op jit(solution)/shard_map/ppermute | solution.py:204
  79.7 0.7 add.7
Async XLA Ops:
  23.5 4.2 %collective-permute-start = (f32[4096,128]{1,0:T(8,128)S(1)}, f32[4096,128]{1,0:T(8,128)S(1)}, u32[]{:S(2)}, u32[]{:S(2)}) collective-permute-start(f32[4096,128]{1,0:T(8,128)S(1)} %get-tuple-element.10), channel_id=1, source_target_pairs={{0,32},{32,0},{64,96},{96,64},{1,33},{33,1},{65,97},{97,65},{2,34}... | collective-permute-start | bytes 6291464 | tf_op jit(solution)/shard_map/ppermute | solution.py:199
  29.4 40.9 %all-to-all-start = ((f32[32,128,128]{2,1,0:T(8,128)}), f32[32,128,128]{2,1,0:T(8,128)S(1)}, u32[]{:S(2)}, u32[]{:S(2)}) async-start(f32[32,128,128]{2,1,0:T(8,128)} %bitcast.6), calls=%async_computation | async-start | bytes 4194304 | tf_op jit(solution)/shard_map/all_to_all | solution.py:201
  72.3 7.4 %collective-permute-start.1 = (f32[2,2,128,128]{3,2,1,0:T(8,128)S(1)}, f32[2,2,128,128]{3,2,1,0:T(8,128)S(1)}, u32[]{:S(2)}, u32[]{:S(2)}) collective-permute-start(f32[2,2,128,128]{3,2,1,0:T(8,128)S(1)} %get-tuple-element.12), channel_id=1, source_target_pairs={{0,64},{32,96},{64,0},{96,32},{1,65},{33,97},{65,1},{97,33},{2,66}... | collective-permute-start | bytes 786440 | tf_op jit(solution)/shard_map/ppermute | solution.py:204
where the time goes:
time: 80.8 us; the launch traced here: 80.4 us
  waiting for transfers between devices  38.2 us (47%)
  Pallas kernels  22.8 us (28%)
  starting transfers between devices  13.5 us (17%)
  other arithmetic  3.84 us (5%)
  local copies, waits for them, and re-layouts  1.38 us (2%)
    all_to_all x1, waiting for transfers between devices, on_device(): lax.all_to_all(mine, 'col', split_axis=0, concat_axis=0, tiled=True)  29.2 us
    pallas_call x1, Pallas kernels, spectrum_call(): pl.pallas_call(spectrum_kernel, out_shape=(out, out), in_specs=[pl.BlockS...  20.8 us
    all_to_all x1, starting transfers between devices, on_device(): lax.all_to_all(mine, 'col', split_axis=0, concat_axis=0, tiled=True)  10.9 us
    ppermute x1, waiting for transfers between devices, on_device(): got = lax.ppermute(send, 'grp', [(i, i ^ 2) for i in range(4)])  4.85 us
    ppermute x1, waiting for transfers between devices, on_device(): got = lax.ppermute(send, 'grp', [(i, i ^ 1) for i in range(4)])  4.15 us
    ppermute x1, starting transfers between devices, on_device(): got = lax.ppermute(send, 'grp', [(i, i ^ 2) for i in range(4)])  2.51 us
    pallas_call x1, Pallas kernels, focal_call(): pl.pallas_call(focal_kernel, out_shape=(out, out), in_specs=[pl.BlockSpec...  2.01 us
    add x1, other arithmetic, on_device(): mine = (keep + got).reshape(32, 128, 128)  1.62 us
  transfers between devices with their start and end apart: 3, of which 3 were waited for; matrix products, arithmetic and copies ran while one was open for 1% of the time, Pallas kernels for 0%

commit v1 on v0

v1 whole, which is shorter than its diff:
```python
import functools
import math

import jax
import jax.numpy as jnp
from jax import lax
from jax.experimental import pallas as pl
from jax.experimental.pallas import tpu as pltpu
from jax.sharding import PartitionSpec as P

NR = 512
NC = 512
NT = 2048
NB = 256
CROP = 128
HALF = NT // 2
TURN = 2048
F32 = jnp.float32
BF16 = jnp.bfloat16


def cos_sin(u):
    v = u + 256
    quadrant = (v >> 9) & 3
    r = ((v & 511) - 256).astype(F32) * (2.0 * math.pi / TURN)
    z = r * r
    s = r + r * z * (-1.6666654611e-1 + z * (8.3321608736e-3 + z * -1.9515295891e-4))
    c = 1.0 - 0.5 * z + z * z * (4.166664568298827e-2 + z * (-1.388731625493765e-3 + z * 2.443315711809948e-5))
    odd = (quadrant & 1) == 1
    cos = jnp.where(odd, s, c)
    sin = jnp.where(odd, c, s)
    cos = jnp.where((quadrant == 1) | (quadrant == 2), -cos, cos)
    sin = jnp.where(quadrant >= 2, -sin, sin)
    return cos, sin


def split(a):
    hi = a.astype(BF16)
    return hi, (a - hi.astype(F32)).astype(BF16)


def dot(a, b, dims):
    return lax.dot_general(a, b, (dims, ((), ())), preferred_element_type=F32)


def dot3(a, b, dims):
    return dot(a[0], b[0], dims) + (dot(a[0], b[1], dims) + dot(a[1], b[0], dims))


NT_DIMS = ((1,), (1,))
NN_DIMS = ((1,), (0,))
TN_DIMS = ((0,), (0,))


PAD = 136
CHUNKS = 4
CROWS = 2048 // CHUNKS


def spectrum_kernel(start_ref, crop_ref, x_hbm, send_ref, keep_ref, xbuf, tab_hi, tab_lo, row_hi, row_lo, sums, sem):
    grp = lax.axis_index("grp")
    start, crop, core, row0 = start_ref[0], crop_ref[0], grp & 1, grp * 128
    copies = []
    for h in range(CHUNKS):
        rows = pl.ds(CROWS * h, CROWS)
        cp = pltpu.make_async_copy(x_hbm.at[rows], xbuf.at[rows], sem.at[h])
        cp.start()
        copies.append(cp)

    flip = start & 1
    scale = 1.0 / math.sqrt(NT)

    def one_table(i, _):
        t = i * 64 + lax.broadcasted_iota(jnp.int32, (64, 128), 0)
        m = lax.broadcasted_iota(jnp.int32, (64, 128), 1)
        owner = jnp.where(m < 64, 1 - core, core)
        j = (m & 32) * 2 + owner * 32 + (m & 31)
        rows = pl.ds(pl.multiple_of(i * 64, 64), 64)
        for e in range(2):
            cos, sin = cos_sin(((start + 2 * j + (e ^ flip)) * t) & (TURN - 1))
            for part, val in ((0, cos * scale), (1, sin * -scale)):
                hi, lo = split(val)
                lanes = slice(256 * e + 128 * part, 256 * e + 128 * part + 128)
                tab_hi[rows, lanes] = hi
                tab_lo[rows, lanes] = lo
        return 0

    lax.fori_loop(0, 16, one_table, 0)

    rscale = 1.0 / math.sqrt(NR)
    r = row0 + lax.broadcasted_iota(jnp.int32, (128, CROP), 0)
    p = crop + lax.broadcasted_iota(jnp.int32, (128, CROP), 1)
    cos, sin = cos_sin(((r * p) & (NR - 1)) * (TURN // NR))
    cos, sin = cos * rscale, sin * rscale
    for rows, cols, val in ((0, 0, cos), (0, 128, -sin), (128, 0, sin), (128, 128, cos)):
        hi, lo = split(val)
        row_hi[rows : rows + 128, cols : cols + 128] = hi
        row_lo[rows : rows + 128, cols : cols + 128] = lo

    for h in range(CHUNKS):
        copies[h].wait()

        def delays(i, _):
            first = h * CROWS + i * 256
            rows = pl.ds(pl.multiple_of(first, 256), 256)
            a = xbuf[rows, 0:HALF]
            b = xbuf[rows, HALF:NT]
            for e in range(2):
                y = split(a + b if e == 0 else a - b)
                d = dot3(y, (tab_hi[:, 256 * e : 256 * e + 256], tab_lo[:, 256 * e : 256 * e + 256]), NN_DIMS)
                d = d.reshape(16, 2, 8, 256)
                at = pl.ds(pl.multiple_of(first // 2, 128), 128)
                for o in range(2):
                    for ri in range(2):
                        sums[e, o, ri, at, :] = d[:, o, :, 128 * ri : 128 * ri + 128].reshape(128, 128)
            return 0

        lax.fori_loop(0, CROWS // 256, delays, 0, unroll=2)

    def rowwise(i, _):
        for e in range(2):
            blocks = []
            for k in range(2):
                c = 2 * i + k
                s = [sums[e, c >> 3, ri, pl.ds(c & 7, 128, stride=8), :] for ri in range(2)]
                blocks.append(jnp.concatenate([s[0].T, s[1].T], axis=1))
            g = dot3(split(jnp.concatenate(blocks, axis=0)), (row_hi[...], row_lo[...]), NN_DIMS)
            for k in range(2):
                first = (e ^ flip) * 32 + 2 * i + k
                for rel, ref in ((0, send_ref), (1, keep_ref)):
                    for y in range(2):
                        at = k * 128 + rel * 64 + y * 32
                        for ri in range(2):
                            ref[pl.ds(y * 64 + ri * 16 + first, 32, stride=PAD), :] = g[
                                at : at + 32, 128 * ri : 128 * ri + 128
                            ]
        return 0

    lax.fori_loop(0, 8, rowwise, 0, unroll=4)


def spectrum_call(start, crop, x):
    out = jax.ShapeDtypeStruct((32 * PAD, 128), F32)
    smem = pl.BlockSpec(memory_space=pltpu.SMEM)
    return pl.pallas_call(
        spectrum_kernel,
        out_shape=(out, out),
        in_specs=[smem, smem, pl.BlockSpec(memory_space=pl.ANY)],
        out_specs=(pl.BlockSpec(memory_space=pltpu.VMEM), pl.BlockSpec(memory_space=pltpu.VMEM)),
        scratch_shapes=[
            pltpu.VMEM((2048, NT), F32),
            pltpu.VMEM((HALF, 512), BF16),
            pltpu.VMEM((HALF, 512), BF16),
            pltpu.VMEM((256, 256), BF16),
            pltpu.VMEM((256, 256), BF16),
            pltpu.VMEM((2, 2, 2, 1024, 128), F32),
            pltpu.SemaphoreType.DMA((CHUNKS,)),
        ],
        compiler_params=pltpu.CompilerParams(vmem_limit_bytes=48 * 2**20),
        name="spectrum",
    )(start, crop, x.reshape(2048, NT))


def focal_kernel(crop_ref, g_ref, send_ref, keep_ref, tab_hi, tab_lo):
    crop, mine = crop_ref[1], lax.axis_index("grp") >> 1
    scale = 1.0 / math.sqrt(NC)
    c = lax.broadcasted_iota(jnp.int32, (NC, CROP), 0)
    q = crop + lax.broadcasted_iota(jnp.int32, (NC, CROP), 1)
    cos, sin = cos_sin(((c * q) & (NC - 1)) * (TURN // NC))
    for lane, val in ((0, cos * scale), (128, sin * scale)):
        hi, lo = split(val)
        tab_hi[:, lane : lane + 128] = hi
        tab_lo[:, lane : lane + 128] = lo
    for rel, ref in ((0, send_ref), (1, keep_ref)):
        y = 1 - mine if rel == 0 else mine
        for e in range(2):
            g = [g_ref[:, y, e, ri, :, :].reshape(NC, CROP) for ri in range(2)]
            g = jnp.concatenate(g, axis=1)
            u = dot3(split(g), (tab_hi[...], tab_lo[...]), TN_DIMS)
            ref[0, e] = u[0:128, 0:128] + u[128:256, 128:256]
            ref[1, e] = u[128:256, 0:128] - u[0:128, 128:256]


def focal_call(crop, g):
    out = jax.ShapeDtypeStruct((2, 2, CROP, CROP), F32)
    return pl.pallas_call(
        focal_kernel,
        out_shape=(out, out),
        in_specs=[pl.BlockSpec(memory_space=pltpu.SMEM), pl.BlockSpec(memory_space=pltpu.VMEM)],
        out_specs=(pl.BlockSpec(memory_space=pltpu.VMEM), pl.BlockSpec(memory_space=pltpu.VMEM)),
        scratch_shapes=[pltpu.VMEM((NC, 256), BF16), pltpu.VMEM((NC, 256), BF16)],
        compiler_params=pltpu.CompilerParams(vmem_limit_bytes=24 * 2**20),
        name="focal",
    )(crop, g)


def on_device(interferogram, sideband_start, crop_start):
    send, keep = spectrum_call(sideband_start, crop_start, interferogram)
    got = lax.ppermute(send, "grp", [(i, i ^ 1) for i in range(4)])
    mine = (keep.reshape(32, PAD, 128) + got.reshape(32, PAD, 128))[:, :128]
    gathered = lax.all_to_all(mine, "col", split_axis=0, concat_axis=0, tiled=True)
    send, keep = focal_call(crop_start, gathered.reshape(32, 2, 2, 2, 16, 128))
    got = lax.ppermute(send, "grp", [(i, i ^ 2) for i in range(4)])
    return keep + got


def solution(mesh):
    return jax.shard_map(
        on_device,
        mesh=mesh,
        in_specs=(P("grp", "col", None), P(), P()),
        out_specs=P(None, ("grp", "col"), None, None),
        check_vma=False,
    )
```

time: 80.8 us -> 69 us (0.85)
  blocking collectives: 0 us -> 40 us
  waiting for transfers between devices: 38.2 us -> 10.5 us
  starting transfers between devices: 13.5 us -> 0.84 us
  Pallas kernels: 22.8 us -> 14.9 us
  other arithmetic: 3.84 us -> 0.96 us
    all_to_all x0 -> x1, blocking collectives: none -> 40 us  [on_device(): lax.all_to_all(mine, 'col', split_axis=0, concat_axis=0, tiled=True)]
    all_to_all x1 -> x0, waiting for transfers between devices: 29.2 us -> none  [on_device(): lax.all_to_all(mine, 'col', split_axis=0, concat_axis=0, tiled=True)]
    all_to_all x1 -> x0, starting transfers between devices: 10.9 us -> none  [on_device(): lax.all_to_all(mine, 'col', split_axis=0, concat_axis=0, tiled=True)]
    pallas_call x1, Pallas kernels: 20.8 us -> 12.8 us  [spectrum_call(): pl.pallas_call(spectrum_kernel, out_shape=(out, out), in_specs=[smem, sme...]
    ppermute x1, starting transfers between devices: 2.51 us -> 0.76 us  [on_device(): got = lax.ppermute(send, 'grp', [(i, i ^ 2) for i in range(4)])]
    another operation x2 -> x0, other arithmetic: 1.47 us -> none  [the longest x1 0.75 us: on_device(): scal = jnp.stack([crop_start[1], y_lo]).astype(jnp.int32)]
    add x1, other arithmetic: 1.62 us -> 0.23 us  [on_device(): mine = (keep.reshape(32, PAD, 128) + got.reshape(32, PAD, 128))[:, :128]]
    ppermute x1, waiting for transfers between devices: 4.85 us -> 6.17 us  [on_device(): got = lax.ppermute(send, 'grp', [(i, i ^ 2) for i in range(4)])]
  transfers between devices with their start and end apart: 3 -> 2, of which waited for: 3 -> 2; matrix products, arithmetic and copies ran while one was open for 1% -> 0% of each run, Pallas kernels for 0% -> 0%
where the time goes in v1:
time: 69 us; the launch traced here: 68.8 us
  blocking collectives  40 us (58%)
  Pallas kernels  14.9 us (22%)
  waiting for transfers between devices  10.5 us (15%)
  other arithmetic  0.96 us (1%)
  local copies, waits for them, and re-layouts  0.89 us (1%)
  starting transfers between devices  0.84 us (1%)
  between operations  0.7 us (1%)
    all_to_all x1, blocking collectives, on_device(): lax.all_to_all(mine, 'col', split_axis=0, concat_axis=0, tiled=True)  40 us
    pallas_call x1, Pallas kernels, spectrum_call(): pl.pallas_call(spectrum_kernel, out_shape=(out, out), in_specs=[smem, sme...  12.8 us
    ppermute x1, waiting for transfers between devices, on_device(): got = lax.ppermute(send, 'grp', [(i, i ^ 2) for i in range(4)])  6.17 us
    ppermute x1, waiting for transfers between devices, on_device(): got = lax.ppermute(send, 'grp', [(i, i ^ 1) for i in range(4)])  4.33 us
    pallas_call x1, Pallas kernels, focal_call(): pl.pallas_call(focal_kernel, out_shape=(out, out), in_specs=[pl.BlockSpec...  2.03 us
  transfers between devices with their start and end apart: 2, of which 2 were waited for; matrix products, arithmetic and copies ran while one was open for 0% of the time, Pallas kernels for 0%

profile of v1, /device:TPU:0, one launch (start us, length us, event | category | flops | bytes accessed | tf_op | source)
XLA Modules:
  0.0 68.8 jit_solution(17178564301539610038)
XLA Ops:
  0.7 0.0 copy-start
  0.7 0.6 copy-done
  1.3 12.8 %spectrum.1 = (f32[4352,128]{1,0:T(8,128)S(1)}, f32[4352,128]{1,0:T(8,128)S(1)}) custom-call(s32[1]{0:T(128)S(6)} %copy.4.start_ref, s32[2]{0:T(128)S(1)} %copy-done, f32[2048,2048]{1,0:T(8,128)} %bitcast.4), custom_call_target="tpu_custom_call" | custom-call | tf_op jit(solution)/shard_map/spectrum/pallas_call | solution.py:145
  14.2 0.1 collective-permute-start
  14.3 4.3 %collective-permute-done = f32[4352,128]{1,0:T(8,128)S(1)} collective-permute-done((f32[4352,128]{1,0:T(8,128)S(1)}, f32[4352,128]{1,0:T(8,128)S(1)}, u32[]{:S(2)}, u32[]{:S(2)}) %collective-permute-start) | collective-permute-done | bytes 2228256 | tf_op jit(solution)/shard_map/ppermute | solution.py:199
  18.6 0.2 add.9
  18.8 0.2 slice.4
  19.1 40.0 %all_to_all.5 = f32[32,128,128]{2,1,0:T(8,128)S(1)} all-to-all(f32[32,128,128]{2,1,0:T(8,128)S(1)} %slice.4), channel_id=1, replica_groups=mesh['grp'=4,'col'=32] {'col'}, dimensions={0} | all-to-all | bytes 4194304 | tf_op jit(solution)/shard_map/all_to_all | solution.py:201
  59.1 2.0 %focal.1 = (f32[2,2,128,128]{3,2,1,0:T(8,128)S(1)}, f32[2,2,128,128]{3,2,1,0:T(8,128)S(1)}) custom-call(s32[2]{0:T(128)S(1)} %copy-done, f32[32,2,2,2,16,128]{5,4,3,2,1,0:T(8,128)S(1)} %bitcast.3), custom_call_target="tpu_custom_call" | custom-call | tf_op jit(solution)/shard_map/focal/pallas_call | solution.py:186
  61.2 0.8 %collective-permute-start.1 = (f32[2,2,128,128]{3,2,1,0:T(8,128)S(1)}, f32[2,2,128,128]{3,2,1,0:T(8,128)S(1)}, u32[]{:S(2)}, u32[]{:S(2)}) collective-permute-start(f32[2,2,128,128]{3,2,1,0:T(8,128)S(1)} %get-tuple-element.12), channel_id=1, source_target_pairs={{0,64},{32,96},{64,0},{96,32},{1,65},{33,97},{65,1},{97,33},{2,66}... | collective-permute-start | bytes 786440 | tf_op jit(solution)/shard_map/ppermute | solution.py:203
  61.9 6.2 %collective-permute-done.1 = f32[2,2,128,128]{3,2,1,0:T(8,128)S(1)} collective-permute-done((f32[2,2,128,128]{3,2,1,0:T(8,128)S(1)}, f32[2,2,128,128]{3,2,1,0:T(8,128)S(1)}, u32[]{:S(2)}, u32[]{:S(2)}) %collective-permute-start.1) | collective-permute-done | bytes 262176 | tf_op jit(solution)/shard_map/ppermute | solution.py:203
  68.1 0.7 %add.11 = f32[2,2,128,128]{3,2,1,0:T(8,128)} add(f32[2,2,128,128]{3,2,1,0:T(8,128)S(1)} %get-tuple-element.11, f32[2,2,128,128]{3,2,1,0:T(8,128)S(1)} %collective-permute-done.1) | non-fusion elementwise | flops 65536 | bytes 786432 | tf_op jit(solution)/shard_map/add | solution.py:204
Async XLA Ops:
  0.7 0.7 copy-start
  14.2 4.4 %collective-permute-start = (f32[4352,128]{1,0:T(8,128)S(1)}, f32[4352,128]{1,0:T(8,128)S(1)}, u32[]{:S(2)}, u32[]{:S(2)}) collective-permute-start(f32[4352,128]{1,0:T(8,128)S(1)} %get-tuple-element.10), channel_id=1, source_target_pairs={{0,32},{32,0},{64,96},{96,64},{1,33},{33,1},{65,97},{97,65},{2,34}... | collective-permute-start | bytes 6684680 | tf_op jit(solution)/shard_map/ppermute | solution.py:199
  61.2 6.9 %collective-permute-start.1 = (f32[2,2,128,128]{3,2,1,0:T(8,128)S(1)}, f32[2,2,128,128]{3,2,1,0:T(8,128)S(1)}, u32[]{:S(2)}, u32[]{:S(2)}) collective-permute-start(f32[2,2,128,128]{3,2,1,0:T(8,128)S(1)} %get-tuple-element.12), channel_id=1, source_target_pairs={{0,64},{32,96},{64,0},{96,32},{1,65},{33,97},{65,1},{97,33},{2,66}... | collective-permute-start | bytes 786440 | tf_op jit(solution)/shard_map/ppermute | solution.py:203

commit v2 on v1

--- a/solution.py
+++ b/solution.py
@@ -57,9 +57,12 @@
 CROWS = 2048 // CHUNKS
 
 
-def spectrum_kernel(start_ref, crop_ref, x_hbm, send_ref, keep_ref, xbuf, tab_hi, tab_lo, row_hi, row_lo, sums, sem):
+def spectrum_kernel(
+    start_ref, crop_ref, x_hbm, send_ref, keep_ref, xbuf, tab_hi, tab_lo, row_hi, row_lo, sums, sem
+):
     grp = lax.axis_index("grp")
-    start, crop, core, row0 = start_ref[0], crop_ref[0], grp & 1, grp * 128
+    start, crop = start_ref[0], crop_ref[0]
+    core, y_lo, row0 = grp & 1, grp >> 1, grp * 128
     copies = []
     for h in range(CHUNKS):
         rows = pl.ds(CROWS * h, CROWS)
@@ -74,10 +77,13 @@
         t = i * 64 + lax.broadcasted_iota(jnp.int32, (64, 128), 0)
         m = lax.broadcasted_iota(jnp.int32, (64, 128), 1)
         owner = jnp.where(m < 64, 1 - core, core)
-        j = (m & 32) * 2 + owner * 32 + (m & 31)
+        other = (m & 32) == 0
+        half = jnp.where(other, 1 - y_lo, y_lo) * 64 + owner * 32
         rows = pl.ds(pl.multiple_of(i * 64, 64), 64)
         for e in range(2):
-            cos, sin = cos_sin(((start + 2 * j + (e ^ flip)) * t) & (TURN - 1))
+            odd = e ^ flip
+            j = half + ((m & 31) ^ jnp.where(other, odd * 16, 0))
+            cos, sin = cos_sin(((start + 2 * j + odd) * t) & (TURN - 1))
             for part, val in ((0, cos * scale), (1, sin * -scale)):
                 hi, lo = split(val)
                 lanes = slice(256 * e + 128 * part, 256 * e + 128 * part + 128)
@@ -161,47 +167,89 @@
     )(start, crop, x.reshape(2048, NT))
 
 
-def focal_kernel(crop_ref, g_ref, send_ref, keep_ref, tab_hi, tab_lo):
-    crop, mine = crop_ref[1], lax.axis_index("grp") >> 1
+def table_kernel(crop_ref, hi_ref, lo_ref):
     scale = 1.0 / math.sqrt(NC)
     c = lax.broadcasted_iota(jnp.int32, (NC, CROP), 0)
-    q = crop + lax.broadcasted_iota(jnp.int32, (NC, CROP), 1)
+    q = crop_ref[1] + lax.broadcasted_iota(jnp.int32, (NC, CROP), 1)
     cos, sin = cos_sin(((c * q) & (NC - 1)) * (TURN // NC))
     for lane, val in ((0, cos * scale), (128, sin * scale)):
         hi, lo = split(val)
-        tab_hi[:, lane : lane + 128] = hi
-        tab_lo[:, lane : lane + 128] = lo
-    for rel, ref in ((0, send_ref), (1, keep_ref)):
-        y = 1 - mine if rel == 0 else mine
-        for e in range(2):
-            g = [g_ref[:, y, e, ri, :, :].reshape(NC, CROP) for ri in range(2)]
-            g = jnp.concatenate(g, axis=1)
-            u = dot3(split(g), (tab_hi[...], tab_lo[...]), TN_DIMS)
-            ref[0, e] = u[0:128, 0:128] + u[128:256, 128:256]
-            ref[1, e] = u[128:256, 0:128] - u[0:128, 128:256]
-
-
-def focal_call(crop, g):
-    out = jax.ShapeDtypeStruct((2, 2, CROP, CROP), F32)
-    return pl.pallas_call(
-        focal_kernel,
+        hi_ref[:, lane : lane + 128] = hi
+        lo_ref[:, lane : lane + 128] = lo
+
+
+def table_call(crop):
+    out = jax.ShapeDtypeStruct((NC, 256), BF16)
+    return pl.pallas_call(
+        table_kernel,
         out_shape=(out, out),
-        in_specs=[pl.BlockSpec(memory_space=pltpu.SMEM), pl.BlockSpec(memory_space=pltpu.VMEM)],
-        out_specs=(pl.BlockSpec(memory_space=pltpu.VMEM), pl.BlockSpec(memory_space=pltpu.VMEM)),
-        scratch_shapes=[pltpu.VMEM((NC, 256), BF16), pltpu.VMEM((NC, 256), BF16)],
+        in_specs=[pl.BlockSpec(memory_space=pltpu.SMEM)],
+        out_specs=(pl.BlockSpec(memory_space=pltpu.VMEM),) * 2,
+        cost_estimate=pl.CostEstimate(flops=4_000_000, bytes_accessed=4_000_000, transcendentals=0),
+        compiler_params=pltpu.CompilerParams(vmem_limit_bytes=8 * 2**20),
+        name="table",
+    )(crop)
+
+
+def focal_kernel(whose, hi_ref, lo_ref, g_ref, *outs):
+    for e in range(2):
+        g = [g_ref[:, whose, e, ri, :, :].reshape(NC, CROP) for ri in range(2)]
+        u = dot3(split(jnp.concatenate(g, axis=1)), (hi_ref[...], lo_ref[...]), TN_DIMS)
+        real = u[0:128, 0:128] + u[128:256, 128:256]
+        imag = u[128:256, 0:128] - u[0:128, 128:256]
+        if len(outs) == 2:
+            outs[e][0], outs[e][1] = real, imag
+        else:
+            outs[0][0, e], outs[0][1, e] = real, imag
+
+
+def focal_call(whose, table, g):
+    if whose == 0:
+        out = (jax.ShapeDtypeStruct((2, CROP, CROP), F32),) * 2
+    else:
+        out = (jax.ShapeDtypeStruct((2, 2, CROP, CROP), F32),)
+    return pl.pallas_call(
+        functools.partial(focal_kernel, whose),
+        out_shape=out,
+        in_specs=[pl.BlockSpec(memory_space=pltpu.VMEM)] * 3,
+        out_specs=(pl.BlockSpec(memory_space=pltpu.VMEM),) * len(out),
+        cost_estimate=pl.CostEstimate(flops=400_000_000, bytes_accessed=4_000_000, transcendentals=0),
         compiler_params=pltpu.CompilerParams(vmem_limit_bytes=24 * 2**20),
-        name="focal",
-    )(crop, g)
+        name="focal_send" if whose == 0 else "focal_keep",
+    )(*table, g)
+
+
+def sum_kernel(keep_ref, even_ref, odd_ref, out_ref):
+    for e, ref in ((0, even_ref), (1, odd_ref)):
+        for ri in range(2):
+            out_ref[ri, e] = keep_ref[ri, e] + ref[ri]
+
+
+def sum_call(keep, even, odd):
+    return pl.pallas_call(
+        sum_kernel,
+        out_shape=jax.ShapeDtypeStruct((2, 2, CROP, CROP), F32),
+        in_specs=[pl.BlockSpec(memory_space=pltpu.VMEM)] * 3,
+        out_specs=pl.BlockSpec(memory_space=pltpu.VMEM),
+        compiler_params=pltpu.CompilerParams(vmem_limit_bytes=4 * 2**20),
+        name="sum",
+    )(keep, even, odd)
 
 
 def on_device(interferogram, sideband_start, crop_start):
     send, keep = spectrum_call(sideband_start, crop_start, interferogram)
     got = lax.ppermute(send, "grp", [(i, i ^ 1) for i in range(4)])
+    got, table = lax.optimization_barrier((got, table_call(crop_start)))
     mine = (keep.reshape(32, PAD, 128) + got.reshape(32, PAD, 128))[:, :128]
     gathered = lax.all_to_all(mine, "col", split_axis=0, concat_axis=0, tiled=True)
-    send, keep = focal_call(crop_start, gathered.reshape(32, 2, 2, 2, 16, 128))
-    got = lax.ppermute(send, "grp", [(i, i ^ 2) for i in range(4)])
-    return keep + got
+    gathered = gathered.reshape(32, 2, 2, 2, 16, 128)
+    even, odd = focal_call(0, table, gathered)
+    near = [(i, i ^ 64) for i in range(128)]
+    far = [(i, i ^ 64 ^ 16) for i in range(128)]
+    even = lax.ppermute(even, ("grp", "col"), near)
+    odd = lax.ppermute(odd, ("grp", "col"), far)
+    (keep,) = focal_call(1, table, gathered)
+    return sum_call(keep, even, odd)
 
 
 def solution(mesh):

time: 69 us -> 67.6 us (0.980)
  waiting for transfers between devices: 10.5 us -> 7.13 us
  starting transfers between devices: 0.84 us -> 2.56 us
  Pallas kernels: 14.9 us -> 15.8 us
  other arithmetic: 0.96 us -> 0.23 us
    ppermute x1 -> x2, waiting for transfers between devices: 6.17 us -> 3.83 us  [the longest x1 1.95 us: on_device(): even = lax.ppermute(even, ('grp', 'col'), near)]
    ppermute x1 -> x2, starting transfers between devices: 0.76 us -> 2.47 us  [the longest x1 1.72 us: on_device(): odd = lax.ppermute(odd, ('grp', 'col'), far)]
    ppermute x1, waiting for transfers between devices: 4.33 us -> 3.3 us  [on_device(): got = lax.ppermute(send, 'grp', [(i, i ^ 1) for i in range(4)])]
    pallas_call x1 -> x4, Pallas kernels: 2.03 us -> 3 us  [the longest x2 1.24 us: focal_call(): pl.pallas_call(functools.partial(focal_kernel, whose), out_shape=out, in_...]
    add x1 -> x0, other arithmetic: 0.73 us -> none  [on_device(): return keep + got]
  transfers between devices with their start and end apart: 2 -> 3, of which waited for: 2 -> 3; matrix products, arithmetic and copies ran while one was open for 0% -> 0% of each run, Pallas kernels for 0% -> 2%
where the time goes in v2:
time: 67.6 us; the launch traced here: 67.4 us
  blocking collectives  40 us (59%)
  Pallas kernels  15.8 us (23%)
  waiting for transfers between devices  7.13 us (11%)
  starting transfers between devices  2.56 us (4%)
  local copies, waits for them, and re-layouts  0.89 us (1%)
  between operations  0.71 us (1%)
    all_to_all x1, blocking collectives, on_device(): lax.all_to_all(mine, 'col', split_axis=0, concat_axis=0, tiled=True)  40 us
    pallas_call x1, Pallas kernels, spectrum_call(): pl.pallas_call(spectrum_kernel, out_shape=(out, out), in_specs=[smem, sme...  12.8 us
    ppermute x1, waiting for transfers between devices, on_device(): got = lax.ppermute(send, 'grp', [(i, i ^ 1) for i in range(4)])  3.3 us
    ppermute x1, waiting for transfers between devices, on_device(): even = lax.ppermute(even, ('grp', 'col'), near)  1.95 us
    ppermute x1, waiting for transfers between devices, on_device(): odd = lax.ppermute(odd, ('grp', 'col'), far)  1.89 us
    ppermute x1, starting transfers between devices, on_device(): odd = lax.ppermute(odd, ('grp', 'col'), far)  1.72 us
  transfers between devices with their start and end apart: 3, of which 3 were waited for; matrix products, arithmetic and copies ran while one was open for 0% of the time, Pallas kernels for 2%

profile of v2, /device:TPU:0, one launch (start us, length us, event | category | flops | bytes accessed | tf_op | source)
XLA Modules:
  0.0 67.4 jit_solution(11808403607652256083)
XLA Ops:
  0.7 0.0 copy-start
  0.7 0.6 copy-done
  1.3 12.8 %spectrum.1 = (f32[4352,128]{1,0:T(8,128)S(1)}, f32[4352,128]{1,0:T(8,128)S(1)}) custom-call(s32[1]{0:T(128)S(6)} %copy.4.start_ref, s32[2]{0:T(128)S(1)} %copy-done, f32[2048,2048]{1,0:T(8,128)} %bitcast.5), custom_call_target="tpu_custom_call" | custom-call | tf_op jit(solution)/shard_map/spectrum/pallas_call | solution.py:151
  14.2 0.1 collective-permute-start
  14.3 1.0 %table.1 = (bf16[512,256]{1,0:T(8,128)(2,1)S(1)}, bf16[512,256]{1,0:T(8,128)(2,1)S(1)}) custom-call(s32[2]{0:T(128)S(1)} %copy-done), custom_call_target="tpu_custom_call" | custom-call | flops 4000000 | bytes 4000000 | tf_op jit(solution)/shard_map/table/pallas_call | solution.py:183
  15.3 3.3 %collective-permute-done = f32[4352,128]{1,0:T(8,128)S(1)} collective-permute-done((f32[4352,128]{1,0:T(8,128)S(1)}, f32[4352,128]{1,0:T(8,128)S(1)}, u32[]{:S(2)}, u32[]{:S(2)}) %collective-permute-start) | collective-permute-done | bytes 2228256 | tf_op jit(solution)/shard_map/ppermute | solution.py:241
  18.6 0.2 add.6
  18.8 0.2 slice.4
  19.1 40.0 %all_to_all.5 = f32[32,128,128]{2,1,0:T(8,128)S(1)} all-to-all(f32[32,128,128]{2,1,0:T(8,128)S(1)} %slice.4), channel_id=1, replica_groups=mesh['grp'=4,'col'=32] {'col'}, dimensions={0} | all-to-all | bytes 4194304 | tf_op jit(solution)/shard_map/all_to_all | solution.py:244
  59.1 0.6 focal_send.1
  59.7 0.8 %collective-permute-start.1 = (f32[2,128,128]{2,1,0:T(8,128)S(1)}, f32[2,128,128]{2,1,0:T(8,128)S(1)}, u32[]{:S(2)}, u32[]{:S(2)}) collective-permute-start(f32[2,128,128]{2,1,0:T(8,128)S(1)} %get-tuple-element.21), channel_id=1, source_target_pairs={{0,64},{1,65},{2,66},{3,67},{4,68},{5,69},{6,70},{7,71},{8,72},{9,... | collective-permute-start | bytes 393224 | tf_op jit(solution)/shard_map/ppermute | solution.py:249
  60.5 1.7 %collective-permute-start.2 = (f32[2,128,128]{2,1,0:T(8,128)S(1)}, f32[2,128,128]{2,1,0:T(8,128)S(1)}, u32[]{:S(2)}, u32[]{:S(2)}) collective-permute-start(f32[2,128,128]{2,1,0:T(8,128)S(1)} %get-tuple-element.22), channel_id=1, source_target_pairs={{0,80},{1,81},{2,82},{3,83},{4,84},{5,85},{6,86},{7,87},{8,88},{9,... | collective-permute-start | bytes 393224 | tf_op jit(solution)/shard_map/ppermute | solution.py:250
  62.2 0.6 focal_keep.1.keep_ref
  62.8 1.9 %collective-permute-done.1.even_ref = f32[2,128,128]{2,1,0:T(8,128)S(1)} collective-permute-done((f32[2,128,128]{2,1,0:T(8,128)S(1)}, f32[2,128,128]{2,1,0:T(8,128)S(1)}, u32[]{:S(2)}, u32[]{:S(2)}) %collective-permute-start.1) | collective-permute-done | bytes 131104 | tf_op jit(solution)/shard_map/ppermute | solution.py:249
  64.8 1.9 %collective-permute-done.2.odd_ref = f32[2,128,128]{2,1,0:T(8,128)S(1)} collective-permute-done((f32[2,128,128]{2,1,0:T(8,128)S(1)}, f32[2,128,128]{2,1,0:T(8,128)S(1)}, u32[]{:S(2)}, u32[]{:S(2)}) %collective-permute-start.2) | collective-permute-done | bytes 131104 | tf_op jit(solution)/shard_map/ppermute | solution.py:250
  66.7 0.7 %sum.1 = f32[2,2,128,128]{3,2,1,0:T(8,128)} custom-call(f32[2,2,128,128]{3,2,1,0:T(8,128)S(1)} %focal_keep.1.keep_ref, f32[2,128,128]{2,1,0:T(8,128)S(1)} %collective-permute-done.1.even_ref, f32[2,128,128]{2,1,0:T(8,128)S(1)} %collective-permute-done.2.odd_ref), custom_call_target="tpu_custom_call" | custom-call | tf_op jit(solution)/shard_map/sum/pallas_call | solution.py:229
Async XLA Ops:
  0.7 0.7 copy-start
  14.2 4.4 %collective-permute-start = (f32[4352,128]{1,0:T(8,128)S(1)}, f32[4352,128]{1,0:T(8,128)S(1)}, u32[]{:S(2)}, u32[]{:S(2)}) collective-permute-start(f32[4352,128]{1,0:T(8,128)S(1)} %get-tuple-element.14), channel_id=1, source_target_pairs={{0,32},{32,0},{64,96},{96,64},{1,33},{33,1},{65,97},{97,65},{2,34}... | collective-permute-start | bytes 6684680 | tf_op jit(solution)/shard_map/ppermute | solution.py:241
  59.7 5.0 %collective-permute-start.1 = (f32[2,128,128]{2,1,0:T(8,128)S(1)}, f32[2,128,128]{2,1,0:T(8,128)S(1)}, u32[]{:S(2)}, u32[]{:S(2)}) collective-permute-start(f32[2,128,128]{2,1,0:T(8,128)S(1)} %get-tuple-element.21), channel_id=1, source_target_pairs={{0,64},{1,65},{2,66},{3,67},{4,68},{5,69},{6,70},{7,71},{8,72},{9,... | collective-permute-start | bytes 393224 | tf_op jit(solution)/shard_map/ppermute | solution.py:249
  60.5 6.2 %collective-permute-start.2 = (f32[2,128,128]{2,1,0:T(8,128)S(1)}, f32[2,128,128]{2,1,0:T(8,128)S(1)}, u32[]{:S(2)}, u32[]{:S(2)}) collective-permute-start(f32[2,128,128]{2,1,0:T(8,128)S(1)} %get-tuple-element.22), channel_id=1, source_target_pairs={{0,80},{1,81},{2,82},{3,83},{4,84},{5,85},{6,86},{7,87},{8,88},{9,... | collective-permute-start | bytes 393224 | tf_op jit(solution)/shard_map/ppermute | solution.py:250

commit v3 on v2

--- a/solution.py
+++ b/solution.py
@@ -13,7 +13,6 @@
 NT = 2048
 NB = 256
 CROP = 128
-HALF = NT // 2
 TURN = 2048
 F32 = jnp.float32
 BF16 = jnp.bfloat16
@@ -53,45 +52,61 @@
 
 
 PAD = 136
-CHUNKS = 4
-CROWS = 2048 // CHUNKS
-
-
-def spectrum_kernel(
-    start_ref, crop_ref, x_hbm, send_ref, keep_ref, xbuf, tab_hi, tab_lo, row_hi, row_lo, sums, sem
-):
+CHUNKS = 2
+CROWS = 128 // CHUNKS
+FOLD = NT // 8
+GROUPS = (((0, 4), 0), ((2, 6), -1), ((1, 7), -1), ((3, 5), 1))
+
+
+def folded(x):
+    s = [x[j] + x[j + 4] for j in range(4)]
+    d = [x[j] - x[j + 4] for j in range(4)]
+    p, q = s[0] + s[2], s[1] + s[3]
+    u, v = (d[1] - d[3]) * math.sqrt(0.5), (d[1] + d[3]) * math.sqrt(0.5)
+    return ((p + q, p - q), (s[0] - s[2], s[1] - s[3]), (d[0] + u, d[2] + v), (d[0] - u, d[2] - v))
+
+
+def spectrum_kernel(start_ref, crop_ref, x_hbm, send_ref, keep_ref, xbuf, table, row_hi, row_lo, sums, sem):
     grp = lax.axis_index("grp")
     start, crop = start_ref[0], crop_ref[0]
     core, y_lo, row0 = grp & 1, grp >> 1, grp * 128
     copies = []
-    for h in range(CHUNKS):
-        rows = pl.ds(CROWS * h, CROWS)
-        cp = pltpu.make_async_copy(x_hbm.at[rows], xbuf.at[rows], sem.at[h])
-        cp.start()
-        copies.append(cp)
-
-    flip = start & 1
+    for o in range(2):
+        for h in range(CHUNKS):
+            rows = pl.ds(CROWS * h, CROWS)
+            cp = pltpu.make_async_copy(x_hbm.at[rows, o], xbuf.at[o, rows], sem.at[o, h])
+            cp.start()
+            copies.append(cp)
+
     scale = 1.0 / math.sqrt(NT)
 
-    def one_table(i, _):
-        t = i * 64 + lax.broadcasted_iota(jnp.int32, (64, 128), 0)
-        m = lax.broadcasted_iota(jnp.int32, (64, 128), 1)
-        owner = jnp.where(m < 64, 1 - core, core)
-        other = (m & 32) == 0
-        half = jnp.where(other, 1 - y_lo, y_lo) * 64 + owner * 32
-        rows = pl.ds(pl.multiple_of(i * 64, 64), 64)
-        for e in range(2):
-            odd = e ^ flip
-            j = half + ((m & 31) ^ jnp.where(other, odd * 16, 0))
-            cos, sin = cos_sin(((start + 2 * j + odd) * t) & (TURN - 1))
-            for part, val in ((0, cos * scale), (1, sin * -scale)):
+    lane = lax.broadcasted_iota(jnp.int32, (1, 128), 1)
+    real, first = lane < 64, (lane & 32) == 0
+    owner = jnp.where((lane & 16) == 0, 1 - core, core)
+    other = (lane & 8) == 0
+    half = jnp.where(other, 1 - y_lo, y_lo)
+    for g, (residues, sign) in enumerate(GROUPS):
+        kappa = (jnp.where(first, residues[0], residues[1]) - start) & 7
+        flip = jnp.where(other, (kappa & 1) * 4, 0)
+        freq = start + kappa + 8 * (half * 16 + owner * 8 + ((lane & 7) ^ flip))
+
+        def one_table(i, _, g=g, sign=sign, freq=freq):
+            t = i * 64 + lax.broadcasted_iota(jnp.int32, (64, 128), 0)
+            cos, sin = cos_sin((freq * t) & (TURN - 1))
+            cos, sin = cos * scale, sin * scale
+            a = jnp.where(real, cos, -sin)
+            if sign == 0:
+                a, b = jnp.where(first, a, 0.0), jnp.where(first, 0.0, a)
+            else:
+                b = jnp.where(real, sin, cos) * jnp.where(first, float(sign), float(-sign))
+            for at, val in ((0, a), (FOLD, b)):
                 hi, lo = split(val)
-                lanes = slice(256 * e + 128 * part, 256 * e + 128 * part + 128)
-                tab_hi[rows, lanes] = hi
-                tab_lo[rows, lanes] = lo
-        return 0
-
-    lax.fori_loop(0, 16, one_table, 0)
+                rows = pl.ds(pl.multiple_of(at + i * 64, 64), 64)
+                table[g, rows, 0:128] = hi
+                table[g, rows, 128:256] = lo
+            return 0
+
+        lax.fori_loop(0, FOLD // 64, one_table, 0)
 
     rscale = 1.0 / math.sqrt(NR)
     r = row0 + lax.broadcasted_iota(jnp.int32, (128, CROP), 0)
@@ -103,46 +118,45 @@
         row_hi[rows : rows + 128, cols : cols + 128] = hi
         row_lo[rows : rows + 128, cols : cols + 128] = lo
 
-    for h in range(CHUNKS):
-        copies[h].wait()
-
-        def delays(i, _):
-            first = h * CROWS + i * 256
-            rows = pl.ds(pl.multiple_of(first, 256), 256)
-            a = xbuf[rows, 0:HALF]
-            b = xbuf[rows, HALF:NT]
-            for e in range(2):
-                y = split(a + b if e == 0 else a - b)
-                d = dot3(y, (tab_hi[:, 256 * e : 256 * e + 256], tab_lo[:, 256 * e : 256 * e + 256]), NN_DIMS)
-                d = d.reshape(16, 2, 8, 256)
-                at = pl.ds(pl.multiple_of(first // 2, 128), 128)
-                for o in range(2):
-                    for ri in range(2):
-                        sums[e, o, ri, at, :] = d[:, o, :, 128 * ri : 128 * ri + 128].reshape(128, 128)
-            return 0
-
-        lax.fori_loop(0, CROWS // 256, delays, 0, unroll=2)
-
-    def rowwise(i, _):
-        for e in range(2):
+    base = []
+    for residues, _ in GROUPS:
+        for residue in residues:
+            kappa = (residue - start) & 7
+            base.append((kappa >> 1) * (8 * PAD) + (kappa & 1) * 32)
+
+    for o in range(2):
+        for h in range(CHUNKS):
+            copies[o * CHUNKS + h].wait()
+            pixels = xbuf.at[o].reshape(1024, NT)
+
+            def delays(i, _, h=h, pixels=pixels):
+                rows = pl.ds(pl.multiple_of(h * CROWS * 8 + i * 256, 256), 256)
+                inputs = folded([pixels[rows, FOLD * j : FOLD * (j + 1)] for j in range(8)])
+                for g in range(4):
+                    hi, lo = split(jnp.concatenate(inputs[g], axis=1))
+                    d = dot(hi, table[g], NN_DIMS) + dot(lo, table[g], NN_DIMS)
+                    sums[g, rows, :] = d[:, 0:128] + d[:, 128:256]
+                return 0
+
+            lax.fori_loop(0, CROWS // 32, delays, 0, unroll=2)
+
+        def rowwise(c, _, o=o):
             blocks = []
-            for k in range(2):
-                c = 2 * i + k
-                s = [sums[e, c >> 3, ri, pl.ds(c & 7, 128, stride=8), :] for ri in range(2)]
-                blocks.append(jnp.concatenate([s[0].T, s[1].T], axis=1))
-            g = dot3(split(jnp.concatenate(blocks, axis=0)), (row_hi[...], row_lo[...]), NN_DIMS)
-            for k in range(2):
-                first = (e ^ flip) * 32 + 2 * i + k
+            for g in range(4):
+                s = sums[g, pl.ds(c, 128, stride=8), :].T
+                blocks.append(jnp.concatenate([s[0:64], s[64:128]], axis=1))
+            f = dot3(split(jnp.concatenate(blocks, axis=0)), (row_hi[...], row_lo[...]), NN_DIMS)
+            for n in range(8):
                 for rel, ref in ((0, send_ref), (1, keep_ref)):
                     for y in range(2):
-                        at = k * 128 + rel * 64 + y * 32
+                        at = n * 32 + rel * 16 + y * 8
                         for ri in range(2):
-                            ref[pl.ds(y * 64 + ri * 16 + first, 32, stride=PAD), :] = g[
-                                at : at + 32, 128 * ri : 128 * ri + 128
+                            ref[pl.ds(base[n] + (y * 64 + ri * 16 + o * 8 + c), 8, stride=PAD), :] = f[
+                                at : at + 8, 128 * ri : 128 * ri + 128
                             ]
-        return 0
-
-    lax.fori_loop(0, 8, rowwise, 0, unroll=4)
+            return 0
+
+        lax.fori_loop(0, 8, rowwise, 0, unroll=True)
 
 
 def spectrum_call(start, crop, x):
@@ -154,17 +168,16 @@
         in_specs=[smem, smem, pl.BlockSpec(memory_space=pl.ANY)],
         out_specs=(pl.BlockSpec(memory_space=pltpu.VMEM), pl.BlockSpec(memory_space=pltpu.VMEM)),
         scratch_shapes=[
-            pltpu.VMEM((2048, NT), F32),
-            pltpu.VMEM((HALF, 512), BF16),
-            pltpu.VMEM((HALF, 512), BF16),
+            pltpu.VMEM((2, 128, 8, NT), F32),
+            pltpu.VMEM((4, 2 * FOLD, 256), BF16),
             pltpu.VMEM((256, 256), BF16),
             pltpu.VMEM((256, 256), BF16),
-            pltpu.VMEM((2, 2, 2, 1024, 128), F32),
-            pltpu.SemaphoreType.DMA((CHUNKS,)),
+            pltpu.VMEM((4, 1024, 128), F32),
+            pltpu.SemaphoreType.DMA((2, CHUNKS)),
         ],
         compiler_params=pltpu.CompilerParams(vmem_limit_bytes=48 * 2**20),
         name="spectrum",
-    )(start, crop, x.reshape(2048, NT))
+    )(start, crop, x.reshape(128, 2, 8, NT))
 
 
 def table_kernel(crop_ref, hi_ref, lo_ref):
@@ -240,7 +253,8 @@
     send, keep = spectrum_call(sideband_start, crop_start, interferogram)
     got = lax.ppermute(send, "grp", [(i, i ^ 1) for i in range(4)])
     got, table = lax.optimization_barrier((got, table_call(crop_start)))
-    mine = (keep.reshape(32, PAD, 128) + got.reshape(32, PAD, 128))[:, :128]
+    mine = (keep + got).reshape(4, 8, PAD, 128)[:, :, :128]
+    mine = mine.transpose(1, 0, 2, 3).reshape(32, 128, 128)
     gathered = lax.all_to_all(mine, "col", split_axis=0, concat_axis=0, tiled=True)
     gathered = gathered.reshape(32, 2, 2, 2, 16, 128)
     even, odd = focal_call(0, table, gathered)

time: 67.6 us -> 65.9 us (0.975)
  Pallas kernels: 15.8 us -> 14 us
    pallas_call x1, Pallas kernels: 12.8 us -> 11.1 us  [spectrum_call(): pl.pallas_call(spectrum_kernel, out_shape=(out, out), in_specs=[smem, sme...]
  transfers between devices with their start and end apart: 3 -> 3, of which waited for: 3 -> 3; matrix products, arithmetic and copies ran while one was open for 0% -> 0% of each run, Pallas kernels for 2% -> 3%
where the time goes in v3:
time: 65.9 us; the launch traced here: 65.8 us
  blocking collectives  40.1 us (61%)
  Pallas kernels  14 us (21%)
  waiting for transfers between devices  7.13 us (11%)
  starting transfers between devices  2.56 us (4%)
  local copies, waits for them, and re-layouts  1.03 us (2%)
  between operations  0.72 us (1%)
    all_to_all x1, blocking collectives, on_device(): lax.all_to_all(mine, 'col', split_axis=0, concat_axis=0, tiled=True)  40.1 us
    pallas_call x1, Pallas kernels, spectrum_call(): pl.pallas_call(spectrum_kernel, out_shape=(out, out), in_specs=[smem, sme...  11.1 us
    ppermute x1, waiting for transfers between devices, on_device(): got = lax.ppermute(send, 'grp', [(i, i ^ 1) for i in range(4)])  3.3 us
    ppermute x1, waiting for transfers between devices, on_device(): even = lax.ppermute(even, ('grp', 'col'), near)  1.95 us
    ppermute x1, waiting for transfers between devices, on_device(): odd = lax.ppermute(odd, ('grp', 'col'), far)  1.89 us
    ppermute x1, starting transfers between devices, on_device(): odd = lax.ppermute(odd, ('grp', 'col'), far)  1.72 us
  transfers between devices with their start and end apart: 3, of which 3 were waited for; matrix products, arithmetic and copies ran while one was open for 0% of the time, Pallas kernels for 3%

profile of v3, /device:TPU:0, one launch (start us, length us, event | category | flops | bytes accessed | tf_op | source)
XLA Modules:
  0.0 65.8 jit_solution(14704028761155157303)
XLA Ops:
  0.7 0.0 copy-start
  0.7 0.6 copy-done
  1.3 11.1 %spectrum.1 = (f32[4352,128]{1,0:T(8,128)S(1)}, f32[4352,128]{1,0:T(8,128)S(1)}) custom-call(s32[1]{0:T(128)S(6)} %copy.5.start_ref, s32[2]{0:T(128)S(1)} %copy-done, f32[128,2,8,2048]{3,2,1,0:T(8,128)} %bitcast.8), custom_call_target="tpu_custom_call" | custom-call | tf_op jit(solution)/shard_map/spectrum/pallas_call | solution.py:165
  12.4 0.1 collective-permute-start
  12.5 1.0 %table.1 = (bf16[512,256]{1,0:T(8,128)(2,1)S(1)}, bf16[512,256]{1,0:T(8,128)(2,1)S(1)}) custom-call(s32[2]{0:T(128)S(1)} %copy-done), custom_call_target="tpu_custom_call" | custom-call | flops 4000000 | bytes 4000000 | tf_op jit(solution)/shard_map/table/pallas_call | solution.py:196
  13.5 3.3 %collective-permute-done = f32[4352,128]{1,0:T(8,128)S(1)} collective-permute-done((f32[4352,128]{1,0:T(8,128)S(1)}, f32[4352,128]{1,0:T(8,128)S(1)}, u32[]{:S(2)}, u32[]{:S(2)}) %collective-permute-start) | collective-permute-done | bytes 2228256 | tf_op jit(solution)/shard_map/ppermute | solution.py:254
  16.8 0.2 add.3
  17.0 0.2 slice_bitcast_fusion
  17.3 0.1 copy.4
  17.4 40.1 %all_to_all.5 = f32[32,128,128]{2,1,0:T(8,128)S(1)} all-to-all(f32[32,128,128]{2,1,0:T(8,128)S(1)} %bitcast.10), channel_id=1, replica_groups=mesh['grp'=4,'col'=32] {'col'}, dimensions={0} | all-to-all | bytes 4194304 | tf_op jit(solution)/shard_map/all_to_all | solution.py:258
  57.5 0.6 focal_send.1
  58.1 0.8 %collective-permute-start.1 = (f32[2,128,128]{2,1,0:T(8,128)S(1)}, f32[2,128,128]{2,1,0:T(8,128)S(1)}, u32[]{:S(2)}, u32[]{:S(2)}) collective-permute-start(f32[2,128,128]{2,1,0:T(8,128)S(1)} %get-tuple-element.21), channel_id=1, source_target_pairs={{0,64},{1,65},{2,66},{3,67},{4,68},{5,69},{6,70},{7,71},{8,72},{9,... | collective-permute-start | bytes 393224 | tf_op jit(solution)/shard_map/ppermute | solution.py:263
  58.9 1.7 %collective-permute-start.2 = (f32[2,128,128]{2,1,0:T(8,128)S(1)}, f32[2,128,128]{2,1,0:T(8,128)S(1)}, u32[]{:S(2)}, u32[]{:S(2)}) collective-permute-start(f32[2,128,128]{2,1,0:T(8,128)S(1)} %get-tuple-element.22), channel_id=1, source_target_pairs={{0,80},{1,81},{2,82},{3,83},{4,84},{5,85},{6,86},{7,87},{8,88},{9,... | collective-permute-start | bytes 393224 | tf_op jit(solution)/shard_map/ppermute | solution.py:264
  60.6 0.6 focal_keep.1.keep_ref
  61.2 1.9 %collective-permute-done.1.even_ref = f32[2,128,128]{2,1,0:T(8,128)S(1)} collective-permute-done((f32[2,128,128]{2,1,0:T(8,128)S(1)}, f32[2,128,128]{2,1,0:T(8,128)S(1)}, u32[]{:S(2)}, u32[]{:S(2)}) %collective-permute-start.1) | collective-permute-done | bytes 131104 | tf_op jit(solution)/shard_map/ppermute | solution.py:263
  63.2 1.9 %collective-permute-done.2.odd_ref = f32[2,128,128]{2,1,0:T(8,128)S(1)} collective-permute-done((f32[2,128,128]{2,1,0:T(8,128)S(1)}, f32[2,128,128]{2,1,0:T(8,128)S(1)}, u32[]{:S(2)}, u32[]{:S(2)}) %collective-permute-start.2) | collective-permute-done | bytes 131104 | tf_op jit(solution)/shard_map/ppermute | solution.py:264
  65.1 0.7 %sum.1 = f32[2,2,128,128]{3,2,1,0:T(8,128)} custom-call(f32[2,2,128,128]{3,2,1,0:T(8,128)S(1)} %focal_keep.1.keep_ref, f32[2,128,128]{2,1,0:T(8,128)S(1)} %collective-permute-done.1.even_ref, f32[2,128,128]{2,1,0:T(8,128)S(1)} %collective-permute-done.2.odd_ref), custom_call_target="tpu_custom_call" | custom-call | tf_op jit(solution)/shard_map/sum/pallas_call | solution.py:242
Async XLA Ops:
  0.7 0.7 copy-start
  12.4 4.4 %collective-permute-start = (f32[4352,128]{1,0:T(8,128)S(1)}, f32[4352,128]{1,0:T(8,128)S(1)}, u32[]{:S(2)}, u32[]{:S(2)}) collective-permute-start(f32[4352,128]{1,0:T(8,128)S(1)} %get-tuple-element.14), channel_id=1, source_target_pairs={{0,32},{32,0},{64,96},{96,64},{1,33},{33,1},{65,97},{97,65},{2,34}... | collective-permute-start | bytes 6684680 | tf_op jit(solution)/shard_map/ppermute | solution.py:254
  58.1 5.0 %collective-permute-start.1 = (f32[2,128,128]{2,1,0:T(8,128)S(1)}, f32[2,128,128]{2,1,0:T(8,128)S(1)}, u32[]{:S(2)}, u32[]{:S(2)}) collective-permute-start(f32[2,128,128]{2,1,0:T(8,128)S(1)} %get-tuple-element.21), channel_id=1, source_target_pairs={{0,64},{1,65},{2,66},{3,67},{4,68},{5,69},{6,70},{7,71},{8,72},{9,... | collective-permute-start | bytes 393224 | tf_op jit(solution)/shard_map/ppermute | solution.py:263
  58.9 6.2 %collective-permute-start.2 = (f32[2,128,128]{2,1,0:T(8,128)S(1)}, f32[2,128,128]{2,1,0:T(8,128)S(1)}, u32[]{:S(2)}, u32[]{:S(2)}) collective-permute-start(f32[2,128,128]{2,1,0:T(8,128)S(1)} %get-tuple-element.22), channel_id=1, source_target_pairs={{0,80},{1,81},{2,82},{3,83},{4,84},{5,85},{6,86},{7,87},{8,88},{9,... | collective-permute-start | bytes 393224 | tf_op jit(solution)/shard_map/ppermute | solution.py:264

commit v4 on v3

--- a/solution.py
+++ b/solution.py
@@ -51,7 +51,6 @@
 TN_DIMS = ((0,), (0,))
 
 
-PAD = 136
 CHUNKS = 2
 CROWS = 128 // CHUNKS
 FOLD = NT // 8
@@ -66,7 +65,35 @@
     return ((p + q, p - q), (s[0] - s[2], s[1] - s[3]), (d[0] + u, d[2] + v), (d[0] - u, d[2] - v))
 
 
-def spectrum_kernel(start_ref, crop_ref, x_hbm, send_ref, keep_ref, xbuf, table, row_hi, row_lo, sums, sem):
+def row_stage(start, sums, row_hi, row_lo, send_ref, keep_ref):
+    base = []
+    for residues, _ in GROUPS:
+        for residue in residues:
+            kappa = (residue - start) & 7
+            base.append((kappa >> 1) * 64 + (kappa & 1) * 512)
+
+    def rowwise(c, _):
+        blocks = []
+        for g in range(4):
+            s = sums[g, pl.ds(c, 128, stride=8), :].T
+            blocks.append(jnp.concatenate([s[0:64], s[64:128]], axis=1))
+        f = dot3(split(jnp.concatenate(blocks, axis=0)), (row_hi[...], row_lo[...]), NN_DIMS)
+        for n in range(8):
+            for rel, ref in ((0, send_ref), (1, keep_ref)):
+                for y in range(2):
+                    at = n * 32 + rel * 16 + y * 8
+                    for ri in range(2):
+                        ref[pl.ds(base[n] + (y * 1024 + ri * 256 + c), 8, stride=8), :] = f[
+                            at : at + 8, 128 * ri : 128 * ri + 128
+                        ]
+        return 0
+
+    lax.fori_loop(0, 8, rowwise, 0, unroll=True)
+
+
+def spectrum_kernel(
+    start_ref, crop_ref, x_hbm, send_ref, keep_ref, later_ref, row_hi, row_lo, xbuf, table, sums, sem
+):
     grp = lax.axis_index("grp")
     start, crop = start_ref[0], crop_ref[0]
     core, y_lo, row0 = grp & 1, grp >> 1, grp * 128
@@ -118,69 +145,88 @@
         row_hi[rows : rows + 128, cols : cols + 128] = hi
         row_lo[rows : rows + 128, cols : cols + 128] = lo
 
-    base = []
-    for residues, _ in GROUPS:
-        for residue in residues:
-            kappa = (residue - start) & 7
-            base.append((kappa >> 1) * (8 * PAD) + (kappa & 1) * 32)
-
-    for o in range(2):
+    for o, spectra in ((0, sums), (1, later_ref)):
         for h in range(CHUNKS):
             copies[o * CHUNKS + h].wait()
             pixels = xbuf.at[o].reshape(1024, NT)
 
-            def delays(i, _, h=h, pixels=pixels):
+            def delays(i, _, h=h, pixels=pixels, spectra=spectra):
                 rows = pl.ds(pl.multiple_of(h * CROWS * 8 + i * 256, 256), 256)
                 inputs = folded([pixels[rows, FOLD * j : FOLD * (j + 1)] for j in range(8)])
                 for g in range(4):
                     hi, lo = split(jnp.concatenate(inputs[g], axis=1))
                     d = dot(hi, table[g], NN_DIMS) + dot(lo, table[g], NN_DIMS)
-                    sums[g, rows, :] = d[:, 0:128] + d[:, 128:256]
+                    spectra[g, rows, :] = d[:, 0:128] + d[:, 128:256]
                 return 0
 
             lax.fori_loop(0, CROWS // 32, delays, 0, unroll=2)
-
-        def rowwise(c, _, o=o):
-            blocks = []
-            for g in range(4):
-                s = sums[g, pl.ds(c, 128, stride=8), :].T
-                blocks.append(jnp.concatenate([s[0:64], s[64:128]], axis=1))
-            f = dot3(split(jnp.concatenate(blocks, axis=0)), (row_hi[...], row_lo[...]), NN_DIMS)
-            for n in range(8):
-                for rel, ref in ((0, send_ref), (1, keep_ref)):
-                    for y in range(2):
-                        at = n * 32 + rel * 16 + y * 8
-                        for ri in range(2):
-                            ref[pl.ds(base[n] + (y * 64 + ri * 16 + o * 8 + c), 8, stride=PAD), :] = f[
-                                at : at + 8, 128 * ri : 128 * ri + 128
-                            ]
-            return 0
-
-        lax.fori_loop(0, 8, rowwise, 0, unroll=True)
+        if o == 0:
+            row_stage(start, sums, row_hi, row_lo, send_ref, keep_ref)
+
+
+VMEM = pl.BlockSpec(memory_space=pltpu.VMEM)
+SMEM = pl.BlockSpec(memory_space=pltpu.SMEM)
+OCTET = jax.ShapeDtypeStruct((2048, 128), F32)
 
 
 def spectrum_call(start, crop, x):
-    out = jax.ShapeDtypeStruct((32 * PAD, 128), F32)
-    smem = pl.BlockSpec(memory_space=pltpu.SMEM)
     return pl.pallas_call(
         spectrum_kernel,
-        out_shape=(out, out),
-        in_specs=[smem, smem, pl.BlockSpec(memory_space=pl.ANY)],
-        out_specs=(pl.BlockSpec(memory_space=pltpu.VMEM), pl.BlockSpec(memory_space=pltpu.VMEM)),
+        out_shape=(
+            OCTET,
+            OCTET,
+            jax.ShapeDtypeStruct((4, 1024, 128), F32),
+            jax.ShapeDtypeStruct((256, 256), BF16),
+            jax.ShapeDtypeStruct((256, 256), BF16),
+        ),
+        in_specs=[SMEM, SMEM, pl.BlockSpec(memory_space=pl.ANY)],
+        out_specs=(VMEM,) * 5,
         scratch_shapes=[
             pltpu.VMEM((2, 128, 8, NT), F32),
             pltpu.VMEM((4, 2 * FOLD, 256), BF16),
-            pltpu.VMEM((256, 256), BF16),
-            pltpu.VMEM((256, 256), BF16),
             pltpu.VMEM((4, 1024, 128), F32),
             pltpu.SemaphoreType.DMA((2, CHUNKS)),
         ],
-        compiler_params=pltpu.CompilerParams(vmem_limit_bytes=48 * 2**20),
+        compiler_params=pltpu.CompilerParams(vmem_limit_bytes=40 * 2**20),
         name="spectrum",
     )(start, crop, x.reshape(128, 2, 8, NT))
 
 
-def table_kernel(crop_ref, hi_ref, lo_ref):
+def row_kernel(start_ref, sums, row_hi, row_lo, send_ref, keep_ref):
+    row_stage(start_ref[0], sums, row_hi, row_lo, send_ref, keep_ref)
+
+
+def row_call(start, sums, row_hi, row_lo):
+    return pl.pallas_call(
+        row_kernel,
+        out_shape=(OCTET, OCTET),
+        in_specs=[SMEM, VMEM, VMEM, VMEM],
+        out_specs=(VMEM, VMEM),
+        cost_estimate=pl.CostEstimate(flops=800_000_000, bytes_accessed=4_000_000, transcendentals=0),
+        compiler_params=pltpu.CompilerParams(vmem_limit_bytes=16 * 2**20),
+        name="rows",
+    )(start, sums, row_hi, row_lo)
+
+
+def assemble_kernel(keep0, got0, keep1, got1, out_ref):
+    for o, (a, b) in enumerate(((keep0, got0), (keep1, got1))):
+        for sub in range(8):
+            out_ref[:, :, sub, o] = (a[sub] + b[sub]).transpose(1, 0, 2, 3)
+
+
+def assemble_call(*parts):
+    return pl.pallas_call(
+        assemble_kernel,
+        out_shape=jax.ShapeDtypeStruct((8, 4, 8, 2, 8, 128), F32),
+        in_specs=[VMEM] * 4,
+        out_specs=VMEM,
+        compiler_params=pltpu.CompilerParams(vmem_limit_bytes=8 * 2**20),
+        name="assemble",
+    )(*(p.reshape(8, 4, 8, 8, 128) for p in parts))
+
+
+def table_kernel(crop_ref, after_ref, hi_ref, lo_ref):
+    del after_ref
     scale = 1.0 / math.sqrt(NC)
     c = lax.broadcasted_iota(jnp.int32, (NC, CROP), 0)
     q = crop_ref[1] + lax.broadcasted_iota(jnp.int32, (NC, CROP), 1)
@@ -191,17 +237,17 @@
         lo_ref[:, lane : lane + 128] = lo
 
 
-def table_call(crop):
+def table_call(crop, after):
     out = jax.ShapeDtypeStruct((NC, 256), BF16)
     return pl.pallas_call(
         table_kernel,
         out_shape=(out, out),
-        in_specs=[pl.BlockSpec(memory_space=pltpu.SMEM)],
+        in_specs=[SMEM, pl.BlockSpec(memory_space=pl.ANY)],
         out_specs=(pl.BlockSpec(memory_space=pltpu.VMEM),) * 2,
         cost_estimate=pl.CostEstimate(flops=4_000_000, bytes_accessed=4_000_000, transcendentals=0),
         compiler_params=pltpu.CompilerParams(vmem_limit_bytes=8 * 2**20),
         name="table",
-    )(crop)
+    )(crop, after)
 
 
 def focal_kernel(whose, hi_ref, lo_ref, g_ref, *outs):
@@ -250,11 +296,13 @@
 
 
 def on_device(interferogram, sideband_start, crop_start):
-    send, keep = spectrum_call(sideband_start, crop_start, interferogram)
-    got = lax.ppermute(send, "grp", [(i, i ^ 1) for i in range(4)])
-    got, table = lax.optimization_barrier((got, table_call(crop_start)))
-    mine = (keep + got).reshape(4, 8, PAD, 128)[:, :, :128]
-    mine = mine.transpose(1, 0, 2, 3).reshape(32, 128, 128)
+    swap = [(i, i ^ 1) for i in range(4)]
+    send0, keep0, later, *row_table = spectrum_call(sideband_start, crop_start, interferogram)
+    got0 = lax.ppermute(send0, "grp", swap)
+    send1, keep1 = row_call(sideband_start, later, *row_table)
+    got1 = lax.ppermute(send1, "grp", swap)
+    got1, table = lax.optimization_barrier((got1, table_call(crop_start, got0)))
+    mine = assemble_call(keep0, got0, keep1, got1).reshape(32, 128, 128)
     gathered = lax.all_to_all(mine, "col", split_axis=0, concat_axis=0, tiled=True)
     gathered = gathered.reshape(32, 2, 2, 2, 16, 128)
     even, odd = focal_call(0, table, gathered)

time: 65.9 us -> 64.5 us (0.979)
  waiting for transfers between devices: 7.13 us -> 5.15 us
    ppermute x1 -> x2, waiting for transfers between devices: 3.3 us -> 1.26 us  [the longest x1 0.79 us: on_device(): got0 = lax.ppermute(send0, 'grp', swap)]
    pallas_call x2 -> x4, Pallas kernels: 12.1 us -> 12.4 us  [the longest x1 9.8 us: spectrum_call(): pl.pallas_call(spectrum_kernel, out_shape=(OCTET, OCTET, jax.ShapeDtypeSt...]
  transfers between devices with their start and end apart: 3 -> 4, of which waited for: 3 -> 4; matrix products, arithmetic and copies ran while one was open for 0% -> 0% of each run, Pallas kernels for 3% -> 5%
where the time goes in v4:
time: 64.5 us; the launch traced here: 64.4 us
  blocking collectives  40.3 us (62%)
  Pallas kernels  14.4 us (22%)
  waiting for transfers between devices  5.15 us (8%)
  starting transfers between devices  3.13 us (5%)
  between operations  0.72 us (1%)
  local copies, waits for them, and re-layouts  0.65 us (1%)
    all_to_all x1, blocking collectives, on_device(): lax.all_to_all(mine, 'col', split_axis=0, concat_axis=0, tiled=True)  40.3 us
    pallas_call x1, Pallas kernels, spectrum_call(): pl.pallas_call(spectrum_kernel, out_shape=(OCTET, OCTET, jax.ShapeDtypeSt...  9.8 us
    ppermute x1, waiting for transfers between devices, on_device(): odd = lax.ppermute(odd, ('grp', 'col'), far)  1.95 us
    ppermute x1, waiting for transfers between devices, on_device(): even = lax.ppermute(even, ('grp', 'col'), near)  1.94 us
    ppermute x1, starting transfers between devices, on_device(): odd = lax.ppermute(odd, ('grp', 'col'), far)  1.65 us
  transfers between devices with their start and end apart: 4, of which 4 were waited for; matrix products, arithmetic and copies ran while one was open for 0% of the time, Pallas kernels for 5%

profile of v4, /device:TPU:0, one launch (start us, length us, event | category | flops | bytes accessed | tf_op | source)
XLA Modules:
  0.0 64.4 jit_solution(4170910444637168457)
XLA Ops:
  0.7 0.0 copy-start
  0.7 0.6 %copy-done = s32[2]{0:T(128)S(1)} copy-done((s32[2]{0:T(128)S(1)}, s32[2]{0:T(128)}, u32[]{:S(2)}) %copy-start) | copy-done | bytes 32
  1.3 9.8 %spectrum.1 = (f32[2048,128]{1,0:T(8,128)S(1)}, f32[2048,128]{1,0:T(8,128)S(1)}, f32[4,1024,128]{2,1,0:T(8,128)S(1)}, bf16[256,256]{1,0:T(8,128)(2,1)S(1)}, bf16[256,256]{1,0:T(8,128)(2,1)S(1)}) custom-call(s32[1]{0:T(128)S(6)} %copy.4.start_ref, s32[2]{0:T(128)S(1)} %copy-done, f32[128,2,8,2048]{3,2,1,0:T(8,128)} %bitcast.14), custom_call_target="tpu_custom_call" | custom-call | tf_op jit(solution)/shard_map/spectrum/pallas_call | solution.py:173
  11.1 0.1 collective-permute-start.1
  11.2 1.3 %rows.1 = (f32[2048,128]{1,0:T(8,128)S(1)}, f32[2048,128]{1,0:T(8,128)S(1)}) custom-call(s32[1]{0:T(128)S(6)} %copy.4.start_ref, f32[4,1024,128]{2,1,0:T(8,128)S(1)} %get-tuple-element.19.sums, bf16[256,256]{1,0:T(8,128)(2,1)S(1)} %get-tuple-element.20.row_hi, bf16[256,256]{1,0:T(8,128)(2,1)S(1)} %get-tuple-element.21.row_lo), custom_call_target="tpu_custom_call" | custom-call | flops 800000000 | bytes 4000000 | tf_op jit(solution)/shard_map/rows/pallas_call | solution.py:200
  12.5 0.6 collective-permute-start
  13.1 0.8 %collective-permute-done.1.after_ref = f32[2048,128]{1,0:T(8,128)S(1)} collective-permute-done((f32[2048,128]{1,0:T(8,128)S(1)}, f32[2048,128]{1,0:T(8,128)S(1)}, u32[]{:S(2)}, u32[]{:S(2)}) %collective-permute-start.1) | collective-permute-done | bytes 1048608 | tf_op jit(solution)/shard_map/ppermute | solution.py:301
  13.9 1.0 %table.1 = (bf16[512,256]{1,0:T(8,128)(2,1)S(1)}, bf16[512,256]{1,0:T(8,128)(2,1)S(1)}) custom-call(s32[2]{0:T(128)S(1)} %copy-done, f32[2048,128]{1,0:T(8,128)S(1)} %collective-permute-done.1.after_ref), custom_call_target="tpu_custom_call" | custom-call | flops 4000000 | bytes 4000000 | tf_op jit(solution)/shard_map/table/pallas_call | solution.py:242
  14.9 0.5 collective-permute-done
  15.4 0.3 assemble.1
  15.7 40.3 %all_to_all.5 = f32[32,128,128]{2,1,0:T(8,128)S(1)} all-to-all(f32[32,128,128]{2,1,0:T(8,128)S(1)} %bitcast.9), channel_id=1, replica_groups=mesh['grp'=4,'col'=32] {'col'}, dimensions={0} | all-to-all | bytes 4194304 | tf_op jit(solution)/shard_map/all_to_all | solution.py:306
  56.0 0.6 focal_send.1
  56.6 0.8 %collective-permute-start.2 = (f32[2,128,128]{2,1,0:T(8,128)S(1)}, f32[2,128,128]{2,1,0:T(8,128)S(1)}, u32[]{:S(2)}, u32[]{:S(2)}) collective-permute-start(f32[2,128,128]{2,1,0:T(8,128)S(1)} %get-tuple-element.31), channel_id=1, source_target_pairs={{0,64},{1,65},{2,66},{3,67},{4,68},{5,69},{6,70},{7,71},{8,72},{9,... | collective-permute-start | bytes 393224 | tf_op jit(solution)/shard_map/ppermute | solution.py:311
  57.4 1.7 %collective-permute-start.3 = (f32[2,128,128]{2,1,0:T(8,128)S(1)}, f32[2,128,128]{2,1,0:T(8,128)S(1)}, u32[]{:S(2)}, u32[]{:S(2)}) collective-permute-start(f32[2,128,128]{2,1,0:T(8,128)S(1)} %get-tuple-element.32), channel_id=1, source_target_pairs={{0,80},{1,81},{2,82},{3,83},{4,84},{5,85},{6,86},{7,87},{8,88},{9,... | collective-permute-start | bytes 393224 | tf_op jit(solution)/shard_map/ppermute | solution.py:312
  59.1 0.6 focal_keep.1.keep_ref
  59.7 1.9 %collective-permute-done.2.even_ref = f32[2,128,128]{2,1,0:T(8,128)S(1)} collective-permute-done((f32[2,128,128]{2,1,0:T(8,128)S(1)}, f32[2,128,128]{2,1,0:T(8,128)S(1)}, u32[]{:S(2)}, u32[]{:S(2)}) %collective-permute-start.2) | collective-permute-done | bytes 131104 | tf_op jit(solution)/shard_map/ppermute | solution.py:311
  61.7 2.0 %collective-permute-done.3.odd_ref = f32[2,128,128]{2,1,0:T(8,128)S(1)} collective-permute-done((f32[2,128,128]{2,1,0:T(8,128)S(1)}, f32[2,128,128]{2,1,0:T(8,128)S(1)}, u32[]{:S(2)}, u32[]{:S(2)}) %collective-permute-start.3) | collective-permute-done | bytes 131104 | tf_op jit(solution)/shard_map/ppermute | solution.py:312
  63.6 0.7 %sum.1 = f32[2,2,128,128]{3,2,1,0:T(8,128)} custom-call(f32[2,2,128,128]{3,2,1,0:T(8,128)S(1)} %focal_keep.1.keep_ref, f32[2,128,128]{2,1,0:T(8,128)S(1)} %collective-permute-done.2.even_ref, f32[2,128,128]{2,1,0:T(8,128)S(1)} %collective-permute-done.3.odd_ref), custom_call_target="tpu_custom_call" | custom-call | tf_op jit(solution)/shard_map/sum/pallas_call | solution.py:288
Async XLA Ops:
  0.7 0.7 %copy-start = (s32[2]{0:T(128)S(1)}, s32[2]{0:T(128)}, u32[]{:S(2)}) copy-start(s32[2]{0:T(128)} %crop_ref.3) | copy-start | bytes 28
  11.1 2.7 %collective-permute-start.1 = (f32[2048,128]{1,0:T(8,128)S(1)}, f32[2048,128]{1,0:T(8,128)S(1)}, u32[]{:S(2)}, u32[]{:S(2)}) collective-permute-start(f32[2048,128]{1,0:T(8,128)S(1)} %get-tuple-element.23), channel_id=1, source_target_pairs={{0,32},{32,0},{64,96},{96,64},{1,33},{33,1},{65,97},{97,65},{2,34}... | collective-permute-start | bytes 3145736 | tf_op jit(solution)/shard_map/ppermute | solution.py:301
  12.5 2.9 %collective-permute-start = (f32[2048,128]{1,0:T(8,128)S(1)}, f32[2048,128]{1,0:T(8,128)S(1)}, u32[]{:S(2)}, u32[]{:S(2)}) collective-permute-start(f32[2048,128]{1,0:T(8,128)S(1)} %get-tuple-element.22), channel_id=1, source_target_pairs={{0,32},{32,0},{64,96},{96,64},{1,33},{33,1},{65,97},{97,65},{2,34}... | collective-permute-start | bytes 3145736 | tf_op jit(solution)/shard_map/ppermute | solution.py:303
  56.6 5.0 %collective-permute-start.2 = (f32[2,128,128]{2,1,0:T(8,128)S(1)}, f32[2,128,128]{2,1,0:T(8,128)S(1)}, u32[]{:S(2)}, u32[]{:S(2)}) collective-permute-start(f32[2,128,128]{2,1,0:T(8,128)S(1)} %get-tuple-element.31), channel_id=1, source_target_pairs={{0,64},{1,65},{2,66},{3,67},{4,68},{5,69},{6,70},{7,71},{8,72},{9,... | collective-permute-start | bytes 393224 | tf_op jit(solution)/shard_map/ppermute | solution.py:311
  57.4 6.2 %collective-permute-start.3 = (f32[2,128,128]{2,1,0:T(8,128)S(1)}, f32[2,128,128]{2,1,0:T(8,128)S(1)}, u32[]{:S(2)}, u32[]{:S(2)}) collective-permute-start(f32[2,128,128]{2,1,0:T(8,128)S(1)} %get-tuple-element.32), channel_id=1, source_target_pairs={{0,80},{1,81},{2,82},{3,83},{4,84},{5,85},{6,86},{7,87},{8,88},{9,... | collective-permute-start | bytes 393224 | tf_op jit(solution)/shard_map/ppermute | solution.py:312

commit v5 on v4

--- a/solution.py
+++ b/solution.py
@@ -6,6 +6,7 @@
 from jax import lax
 from jax.experimental import pallas as pl
 from jax.experimental.pallas import tpu as pltpu
+from jax.sharding import Mesh
 from jax.sharding import PartitionSpec as P
 
 NR = 512
@@ -51,8 +52,7 @@
 TN_DIMS = ((0,), (0,))
 
 
-CHUNKS = 2
-CROWS = 128 // CHUNKS
+CHUNKS = (((0, 32), (32, 32), (64, 64)), ((0, 64), (64, 64)))
 FOLD = NT // 8
 GROUPS = (((0, 4), 0), ((2, 6), -1), ((1, 7), -1), ((3, 5), 1))
 
@@ -94,13 +94,12 @@
 def spectrum_kernel(
     start_ref, crop_ref, x_hbm, send_ref, keep_ref, later_ref, row_hi, row_lo, xbuf, table, sums, sem
 ):
-    grp = lax.axis_index("grp")
-    start, crop = start_ref[0], crop_ref[0]
-    core, y_lo, row0 = grp & 1, grp >> 1, grp * 128
+    core = lax.axis_index("core")
+    start, crop, row0 = start_ref[0], crop_ref[0], (lax.axis_index("half") * 2 + core) * 128
     copies = []
     for o in range(2):
-        for h in range(CHUNKS):
-            rows = pl.ds(CROWS * h, CROWS)
+        for h, chunk in enumerate(CHUNKS[o]):
+            rows = pl.ds(*chunk)
             cp = pltpu.make_async_copy(x_hbm.at[rows, o], xbuf.at[o, rows], sem.at[o, h])
             cp.start()
             copies.append(cp)
@@ -110,12 +109,9 @@
     lane = lax.broadcasted_iota(jnp.int32, (1, 128), 1)
     real, first = lane < 64, (lane & 32) == 0
     owner = jnp.where((lane & 16) == 0, 1 - core, core)
-    other = (lane & 8) == 0
-    half = jnp.where(other, 1 - y_lo, y_lo)
     for g, (residues, sign) in enumerate(GROUPS):
         kappa = (jnp.where(first, residues[0], residues[1]) - start) & 7
-        flip = jnp.where(other, (kappa & 1) * 4, 0)
-        freq = start + kappa + 8 * (half * 16 + owner * 8 + ((lane & 7) ^ flip))
+        freq = start + kappa + 8 * ((lane & 8) * 2 + owner * 8 + (lane & 7))
 
         def one_table(i, _, g=g, sign=sign, freq=freq):
             t = i * 64 + lax.broadcasted_iota(jnp.int32, (64, 128), 0)
@@ -146,12 +142,12 @@
         row_lo[rows : rows + 128, cols : cols + 128] = lo
 
     for o, spectra in ((0, sums), (1, later_ref)):
-        for h in range(CHUNKS):
-            copies[o * CHUNKS + h].wait()
+        for h, (first, count) in enumerate(CHUNKS[o]):
+            copies[3 * o + h].wait()
             pixels = xbuf.at[o].reshape(1024, NT)
 
-            def delays(i, _, h=h, pixels=pixels, spectra=spectra):
-                rows = pl.ds(pl.multiple_of(h * CROWS * 8 + i * 256, 256), 256)
+            def delays(i, _, first=first, pixels=pixels, spectra=spectra):
+                rows = pl.ds(pl.multiple_of(first * 8 + i * 256, 256), 256)
                 inputs = folded([pixels[rows, FOLD * j : FOLD * (j + 1)] for j in range(8)])
                 for g in range(4):
                     hi, lo = split(jnp.concatenate(inputs[g], axis=1))
@@ -159,7 +155,7 @@
                     spectra[g, rows, :] = d[:, 0:128] + d[:, 128:256]
                 return 0
 
-            lax.fori_loop(0, CROWS // 32, delays, 0, unroll=2)
+            lax.fori_loop(0, count // 32, delays, 0, unroll=True)
         if o == 0:
             row_stage(start, sums, row_hi, row_lo, send_ref, keep_ref)
 
@@ -185,7 +181,7 @@
             pltpu.VMEM((2, 128, 8, NT), F32),
             pltpu.VMEM((4, 2 * FOLD, 256), BF16),
             pltpu.VMEM((4, 1024, 128), F32),
-            pltpu.SemaphoreType.DMA((2, CHUNKS)),
+            pltpu.SemaphoreType.DMA((2, 3)),
         ],
         compiler_params=pltpu.CompilerParams(vmem_limit_bytes=40 * 2**20),
         name="spectrum",
@@ -210,19 +206,20 @@
 
 def assemble_kernel(keep0, got0, keep1, got1, out_ref):
     for o, (a, b) in enumerate(((keep0, got0), (keep1, got1))):
-        for sub in range(8):
-            out_ref[:, :, sub, o] = (a[sub] + b[sub]).transpose(1, 0, 2, 3)
+        for y in range(2):
+            for sub in range(4):
+                out_ref[y, :, :, sub, o] = (a[y, sub] + b[y, sub]).transpose(1, 0, 2, 3)
 
 
 def assemble_call(*parts):
     return pl.pallas_call(
         assemble_kernel,
-        out_shape=jax.ShapeDtypeStruct((8, 4, 8, 2, 8, 128), F32),
+        out_shape=jax.ShapeDtypeStruct((2, 8, 4, 4, 2, 8, 128), F32),
         in_specs=[VMEM] * 4,
         out_specs=VMEM,
         compiler_params=pltpu.CompilerParams(vmem_limit_bytes=8 * 2**20),
         name="assemble",
-    )(*(p.reshape(8, 4, 8, 8, 128) for p in parts))
+    )(*(p.reshape(2, 4, 4, 8, 8, 128) for p in parts))
 
 
 def table_kernel(crop_ref, after_ref, hi_ref, lo_ref):
@@ -250,75 +247,43 @@
     )(crop, after)
 
 
-def focal_kernel(whose, hi_ref, lo_ref, g_ref, *outs):
+def focal_kernel(hi_ref, lo_ref, g_ref, out_ref):
     for e in range(2):
-        g = [g_ref[:, whose, e, ri, :, :].reshape(NC, CROP) for ri in range(2)]
+        g = [(g_ref[0:32, 2 * e + ri] + g_ref[32:64, 2 * e + ri]).reshape(NC, CROP) for ri in range(2)]
         u = dot3(split(jnp.concatenate(g, axis=1)), (hi_ref[...], lo_ref[...]), TN_DIMS)
-        real = u[0:128, 0:128] + u[128:256, 128:256]
-        imag = u[128:256, 0:128] - u[0:128, 128:256]
-        if len(outs) == 2:
-            outs[e][0], outs[e][1] = real, imag
-        else:
-            outs[0][0, e], outs[0][1, e] = real, imag
-
-
-def focal_call(whose, table, g):
-    if whose == 0:
-        out = (jax.ShapeDtypeStruct((2, CROP, CROP), F32),) * 2
-    else:
-        out = (jax.ShapeDtypeStruct((2, 2, CROP, CROP), F32),)
-    return pl.pallas_call(
-        functools.partial(focal_kernel, whose),
-        out_shape=out,
-        in_specs=[pl.BlockSpec(memory_space=pltpu.VMEM)] * 3,
-        out_specs=(pl.BlockSpec(memory_space=pltpu.VMEM),) * len(out),
-        cost_estimate=pl.CostEstimate(flops=400_000_000, bytes_accessed=4_000_000, transcendentals=0),
-        compiler_params=pltpu.CompilerParams(vmem_limit_bytes=24 * 2**20),
-        name="focal_send" if whose == 0 else "focal_keep",
+        out_ref[0, e] = u[0:128, 0:128] + u[128:256, 128:256]
+        out_ref[1, e] = u[128:256, 0:128] - u[0:128, 128:256]
+
+
+def focal_call(table, g):
+    return pl.pallas_call(
+        focal_kernel,
+        out_shape=jax.ShapeDtypeStruct((2, 2, CROP, CROP), F32),
+        in_specs=[VMEM] * 3,
+        out_specs=VMEM,
+        compiler_params=pltpu.CompilerParams(vmem_limit_bytes=16 * 2**20),
+        name="focal",
     )(*table, g)
 
 
-def sum_kernel(keep_ref, even_ref, odd_ref, out_ref):
-    for e, ref in ((0, even_ref), (1, odd_ref)):
-        for ri in range(2):
-            out_ref[ri, e] = keep_ref[ri, e] + ref[ri]
-
-
-def sum_call(keep, even, odd):
-    return pl.pallas_call(
-        sum_kernel,
-        out_shape=jax.ShapeDtypeStruct((2, 2, CROP, CROP), F32),
-        in_specs=[pl.BlockSpec(memory_space=pltpu.VMEM)] * 3,
-        out_specs=pl.BlockSpec(memory_space=pltpu.VMEM),
-        compiler_params=pltpu.CompilerParams(vmem_limit_bytes=4 * 2**20),
-        name="sum",
-    )(keep, even, odd)
-
-
 def on_device(interferogram, sideband_start, crop_start):
-    swap = [(i, i ^ 1) for i in range(4)]
+    cores = [(0, 1), (1, 0)]
     send0, keep0, later, *row_table = spectrum_call(sideband_start, crop_start, interferogram)
-    got0 = lax.ppermute(send0, "grp", swap)
+    got0 = lax.ppermute(send0, "core", cores)
     send1, keep1 = row_call(sideband_start, later, *row_table)
-    got1 = lax.ppermute(send1, "grp", swap)
+    got1 = lax.ppermute(send1, "core", cores)
     got1, table = lax.optimization_barrier((got1, table_call(crop_start, got0)))
-    mine = assemble_call(keep0, got0, keep1, got1).reshape(32, 128, 128)
-    gathered = lax.all_to_all(mine, "col", split_axis=0, concat_axis=0, tiled=True)
-    gathered = gathered.reshape(32, 2, 2, 2, 16, 128)
-    even, odd = focal_call(0, table, gathered)
-    near = [(i, i ^ 64) for i in range(128)]
-    far = [(i, i ^ 64 ^ 16) for i in range(128)]
-    even = lax.ppermute(even, ("grp", "col"), near)
-    odd = lax.ppermute(odd, ("grp", "col"), far)
-    (keep,) = focal_call(1, table, gathered)
-    return sum_call(keep, even, odd)
+    mine = assemble_call(keep0, got0, keep1, got1).reshape(64, 64, 128)
+    gathered = lax.all_to_all(mine, ("half", "col"), split_axis=0, concat_axis=0, tiled=True)
+    return focal_call(table, gathered.reshape(64, 4, 16, 128))
 
 
 def solution(mesh):
+    mesh = Mesh(mesh.devices.reshape(2, 2, 32), ("half", "core", "col"))
     return jax.shard_map(
         on_device,
         mesh=mesh,
-        in_specs=(P("grp", "col", None), P(), P()),
-        out_specs=P(None, ("grp", "col"), None, None),
+        in_specs=(P(("half", "core"), "col", None), P(), P()),
+        out_specs=P(None, ("half", "core", "col"), None, None),
         check_vma=False,
     )

time: 64.5 us -> 58.5 us (0.907)
  waiting for transfers between devices: 5.15 us -> 1.25 us
  starting transfers between devices: 3.13 us -> 0.66 us
  blocking collectives: 40.3 us -> 41.4 us
  Pallas kernels: 14.4 us -> 13.6 us
    ppermute x4 -> x2, waiting for transfers between devices: 5.15 us -> 1.25 us  [the longest x1 0.79 us: on_device(): got0 = lax.ppermute(send0, 'core', cores)]
    ppermute x4 -> x2, starting transfers between devices: 3.13 us -> 0.66 us  [the longest x1 0.58 us: on_device(): got1 = lax.ppermute(send1, 'core', cores)]
    all_to_all x1, blocking collectives: 40.3 us -> 41.4 us  [on_device(): lax.all_to_all(mine, ('half', 'col'), split_axis=0, concat_axis=0, tiled=...]
    pallas_call x4 -> x2, Pallas kernels: 2.31 us -> 1.68 us  [the longest x1 1.34 us: focal_call(): pl.pallas_call(focal_kernel, out_shape=jax.ShapeDtypeStruct((2, 2, CROP,...]
  transfers between devices with their start and end apart: 4 -> 2, of which waited for: 4 -> 2; matrix products, arithmetic and copies ran while one was open for 0% -> 0% of each run, Pallas kernels for 5% -> 4%
where the time goes in v5:
time: 58.5 us; the launch traced here: 58.3 us
  blocking collectives  41.4 us (71%)
  Pallas kernels  13.6 us (23%)
  waiting for transfers between devices  1.25 us (2%)
  between operations  0.7 us (1%)
  starting transfers between devices  0.66 us (1%)
  local copies, waits for them, and re-layouts  0.65 us (1%)
    all_to_all x1, blocking collectives, on_device(): lax.all_to_all(mine, ('half', 'col'), split_axis=0, concat_axis=0, tiled=...  41.4 us
    pallas_call x1, Pallas kernels, spectrum_call(): pl.pallas_call(spectrum_kernel, out_shape=(OCTET, OCTET, jax.ShapeDtypeSt...  9.66 us
    pallas_call x1, Pallas kernels, focal_call(): pl.pallas_call(focal_kernel, out_shape=jax.ShapeDtypeStruct((2, 2, CROP,...  1.34 us
    pallas_call x1, Pallas kernels, row_call(): pl.pallas_call(row_kernel, out_shape=(OCTET, OCTET), in_specs=[SMEM, VMEM...  1.27 us
  transfers between devices with their start and end apart: 2, of which 2 were waited for; matrix products, arithmetic and copies ran while one was open for 0% of the time, Pallas kernels for 4%

profile of v5, /device:TPU:0, one launch (start us, length us, event | category | flops | bytes accessed | tf_op | source)
XLA Modules:
  0.0 58.3 jit_solution(8799411774850702263)
XLA Ops:
  0.7 0.0 copy-start
  0.7 0.6 %copy-done = s32[2]{0:T(128)S(1)} copy-done((s32[2]{0:T(128)S(1)}, s32[2]{0:T(128)}, u32[]{:S(2)}) %copy-start) | copy-done | bytes 32
  1.3 9.7 %spectrum.1 = (f32[2048,128]{1,0:T(8,128)S(1)}, f32[2048,128]{1,0:T(8,128)S(1)}, f32[4,1024,128]{2,1,0:T(8,128)S(1)}, bf16[256,256]{1,0:T(8,128)(2,1)S(1)}, bf16[256,256]{1,0:T(8,128)(2,1)S(1)}) custom-call(s32[1]{0:T(128)S(6)} %copy.4.start_ref, s32[2]{0:T(128)S(1)} %copy-done, f32[128,2,8,2048]{3,2,1,0:T(8,128)} %bitcast.13), custom_call_target="tpu_custom_call" | custom-call | tf_op jit(solution)/shard_map/spectrum/pallas_call | solution.py:169
  11.0 0.1 collective-permute-start.1
  11.1 1.3 %rows.1 = (f32[2048,128]{1,0:T(8,128)S(1)}, f32[2048,128]{1,0:T(8,128)S(1)}) custom-call(s32[1]{0:T(128)S(6)} %copy.4.start_ref, f32[4,1024,128]{2,1,0:T(8,128)S(1)} %get-tuple-element.17.sums, bf16[256,256]{1,0:T(8,128)(2,1)S(1)} %get-tuple-element.18.row_hi, bf16[256,256]{1,0:T(8,128)(2,1)S(1)} %get-tuple-element.19.row_lo), custom_call_target="tpu_custom_call" | custom-call | flops 800000000 | bytes 4000000 | tf_op jit(solution)/shard_map/rows/pallas_call | solution.py:196
  12.4 0.6 collective-permute-start
  12.9 0.8 %collective-permute-done.1.after_ref = f32[2048,128]{1,0:T(8,128)S(1)} collective-permute-done((f32[2048,128]{1,0:T(8,128)S(1)}, f32[2048,128]{1,0:T(8,128)S(1)}, u32[]{:S(2)}, u32[]{:S(2)}) %collective-permute-start.1) | collective-permute-done | bytes 1048608 | tf_op jit(solution)/shard_map/ppermute | solution.py:272
  13.7 1.0 %table.1 = (bf16[512,256]{1,0:T(8,128)(2,1)S(1)}, bf16[512,256]{1,0:T(8,128)(2,1)S(1)}) custom-call(s32[2]{0:T(128)S(1)} %copy-done, f32[2048,128]{1,0:T(8,128)S(1)} %collective-permute-done.1.after_ref), custom_call_target="tpu_custom_call" | custom-call | flops 4000000 | bytes 4000000 | tf_op jit(solution)/shard_map/table/pallas_call | solution.py:239
  14.8 0.5 collective-permute-done
  15.2 0.3 assemble.1
  15.6 41.4 %all_to_all.5 = f32[64,64,128]{2,1,0:T(8,128)S(1)} all-to-all(f32[64,64,128]{2,1,0:T(8,128)S(1)} %bitcast.7), channel_id=1, replica_groups=mesh['half'=2,'core'=2,'col'=32] {'half','col'}, dimensions={0} | all-to-all | bytes 4194304 | tf_op jit(solution)/shard_map/all_to_all | solution.py:277
  57.0 1.3 %focal.1 = f32[2,2,128,128]{3,2,1,0:T(8,128)} custom-call(bf16[512,256]{1,0:T(8,128)(2,1)S(1)} %get-tuple-element.24.hi_ref, bf16[512,256]{1,0:T(8,128)(2,1)S(1)} %get-tuple-element.25.lo_ref, f32[64,4,16,128]{3,2,1,0:T(8,128)S(1)} %bitcast.8), custom_call_target="tpu_custom_call" | custom-call | tf_op jit(solution)/shard_map/focal/pallas_call | solution.py:259
Async XLA Ops:
  0.7 0.7 %copy-start = (s32[2]{0:T(128)S(1)}, s32[2]{0:T(128)}, u32[]{:S(2)}) copy-start(s32[2]{0:T(128)} %crop_ref.3) | copy-start | bytes 28
  11.0 2.7 %collective-permute-start.1 = (f32[2048,128]{1,0:T(8,128)S(1)}, f32[2048,128]{1,0:T(8,128)S(1)}, u32[]{:S(2)}, u32[]{:S(2)}) collective-permute-start(f32[2048,128]{1,0:T(8,128)S(1)} %get-tuple-element.21), channel_id=1, source_target_pairs={{0,32},{32,0},{1,33},{33,1},{2,34},{34,2},{3,35},{35,3},{4,36},{36... | collective-permute-start | bytes 3145736 | tf_op jit(solution)/shard_map/ppermute | solution.py:272
  12.4 2.9 %collective-permute-start = (f32[2048,128]{1,0:T(8,128)S(1)}, f32[2048,128]{1,0:T(8,128)S(1)}, u32[]{:S(2)}, u32[]{:S(2)}) collective-permute-start(f32[2048,128]{1,0:T(8,128)S(1)} %get-tuple-element.20), channel_id=1, source_target_pairs={{0,32},{32,0},{1,33},{33,1},{2,34},{34,2},{3,35},{35,3},{4,36},{36... | collective-permute-start | bytes 3145736 | tf_op jit(solution)/shard_map/ppermute | solution.py:274

commit v6 on v5

--- a/solution.py
+++ b/solution.py
@@ -47,12 +47,11 @@
     return dot(a[0], b[0], dims) + (dot(a[0], b[1], dims) + dot(a[1], b[0], dims))
 
 
-NT_DIMS = ((1,), (1,))
 NN_DIMS = ((1,), (0,))
 TN_DIMS = ((0,), (0,))
 
 
-CHUNKS = (((0, 32), (32, 32), (64, 64)), ((0, 64), (64, 64)))
+CHUNKS = (((0, 32), (32, 32), (64, 64)), ((0, 64), (64, 32), (96, 32)))
 FOLD = NT // 8
 GROUPS = (((0, 4), 0), ((2, 6), -1), ((1, 7), -1), ((3, 5), 1))
 
@@ -91,11 +90,8 @@
     lax.fori_loop(0, 8, rowwise, 0, unroll=True)
 
 
-def spectrum_kernel(
-    start_ref, crop_ref, x_hbm, send_ref, keep_ref, later_ref, row_hi, row_lo, xbuf, table, sums, sem
-):
-    core = lax.axis_index("core")
-    start, crop, row0 = start_ref[0], crop_ref[0], (lax.axis_index("half") * 2 + core) * 128
+def spectrum_kernel(start_ref, x_hbm, first_ref, second_ref, xbuf, table, sem):
+    core, start = lax.axis_index("core"), start_ref[0]
     copies = []
     for o in range(2):
         for h, chunk in enumerate(CHUNKS[o]):
@@ -131,6 +127,48 @@
 
         lax.fori_loop(0, FOLD // 64, one_table, 0)
 
+    for o, spectra in ((0, first_ref), (1, second_ref)):
+        for h, (first, count) in enumerate(CHUNKS[o]):
+            copies[3 * o + h].wait()
+            pixels = xbuf.at[o].reshape(1024, NT)
+
+            def delays(i, _, first=first, pixels=pixels, spectra=spectra):
+                rows = pl.ds(pl.multiple_of(first * 8 + i * 256, 256), 256)
+                inputs = folded([pixels[rows, FOLD * j : FOLD * (j + 1)] for j in range(8)])
+                for g in range(4):
+                    hi, lo = split(jnp.concatenate(inputs[g], axis=1))
+                    d = dot(jnp.concatenate([hi, lo], axis=0), table[g], NN_DIMS)
+                    d = d[0:256] + d[256:512]
+                    spectra[g, rows, :] = d[:, 0:128] + d[:, 128:256]
+                return 0
+
+            lax.fori_loop(0, count // 32, delays, 0, unroll=True)
+
+
+VMEM = pl.BlockSpec(memory_space=pltpu.VMEM)
+SMEM = pl.BlockSpec(memory_space=pltpu.SMEM)
+OCTET = jax.ShapeDtypeStruct((2048, 128), F32)
+ROW_TABLE = jax.ShapeDtypeStruct((256, 256), BF16)
+
+
+def spectrum_call(start, x):
+    return pl.pallas_call(
+        spectrum_kernel,
+        out_shape=(jax.ShapeDtypeStruct((4, 1024, 128), F32),) * 2,
+        in_specs=[SMEM, pl.BlockSpec(memory_space=pl.ANY)],
+        out_specs=(VMEM, VMEM),
+        scratch_shapes=[
+            pltpu.VMEM((2, 128, 8, NT), F32),
+            pltpu.VMEM((4, 2 * FOLD, 256), BF16),
+            pltpu.SemaphoreType.DMA((2, 3)),
+        ],
+        compiler_params=pltpu.CompilerParams(vmem_limit_bytes=40 * 2**20),
+        name="spectrum",
+    )(start, x.reshape(128, 2, 8, NT))
+
+
+def first_rows_kernel(start_ref, crop_ref, sums, send_ref, keep_ref, row_hi, row_lo):
+    crop, row0 = crop_ref[0:1, 0:1], (lax.axis_index("half") * 2 + lax.axis_index("core")) * 128
     rscale = 1.0 / math.sqrt(NR)
     r = row0 + lax.broadcasted_iota(jnp.int32, (128, CROP), 0)
     p = crop + lax.broadcasted_iota(jnp.int32, (128, CROP), 1)
@@ -140,67 +178,33 @@
         hi, lo = split(val)
         row_hi[rows : rows + 128, cols : cols + 128] = hi
         row_lo[rows : rows + 128, cols : cols + 128] = lo
-
-    for o, spectra in ((0, sums), (1, later_ref)):
-        for h, (first, count) in enumerate(CHUNKS[o]):
-            copies[3 * o + h].wait()
-            pixels = xbuf.at[o].reshape(1024, NT)
-
-            def delays(i, _, first=first, pixels=pixels, spectra=spectra):
-                rows = pl.ds(pl.multiple_of(first * 8 + i * 256, 256), 256)
-                inputs = folded([pixels[rows, FOLD * j : FOLD * (j + 1)] for j in range(8)])
-                for g in range(4):
-                    hi, lo = split(jnp.concatenate(inputs[g], axis=1))
-                    d = dot(hi, table[g], NN_DIMS) + dot(lo, table[g], NN_DIMS)
-                    spectra[g, rows, :] = d[:, 0:128] + d[:, 128:256]
-                return 0
-
-            lax.fori_loop(0, count // 32, delays, 0, unroll=True)
-        if o == 0:
-            row_stage(start, sums, row_hi, row_lo, send_ref, keep_ref)
-
-
-VMEM = pl.BlockSpec(memory_space=pltpu.VMEM)
-SMEM = pl.BlockSpec(memory_space=pltpu.SMEM)
-OCTET = jax.ShapeDtypeStruct((2048, 128), F32)
-
-
-def spectrum_call(start, crop, x):
-    return pl.pallas_call(
-        spectrum_kernel,
-        out_shape=(
-            OCTET,
-            OCTET,
-            jax.ShapeDtypeStruct((4, 1024, 128), F32),
-            jax.ShapeDtypeStruct((256, 256), BF16),
-            jax.ShapeDtypeStruct((256, 256), BF16),
-        ),
-        in_specs=[SMEM, SMEM, pl.BlockSpec(memory_space=pl.ANY)],
-        out_specs=(VMEM,) * 5,
-        scratch_shapes=[
-            pltpu.VMEM((2, 128, 8, NT), F32),
-            pltpu.VMEM((4, 2 * FOLD, 256), BF16),
-            pltpu.VMEM((4, 1024, 128), F32),
-            pltpu.SemaphoreType.DMA((2, 3)),
-        ],
-        compiler_params=pltpu.CompilerParams(vmem_limit_bytes=40 * 2**20),
-        name="spectrum",
-    )(start, crop, x.reshape(128, 2, 8, NT))
-
-
-def row_kernel(start_ref, sums, row_hi, row_lo, send_ref, keep_ref):
     row_stage(start_ref[0], sums, row_hi, row_lo, send_ref, keep_ref)
 
 
-def row_call(start, sums, row_hi, row_lo):
-    return pl.pallas_call(
-        row_kernel,
+def first_rows_call(start, crop, sums):
+    return pl.pallas_call(
+        first_rows_kernel,
+        out_shape=(OCTET, OCTET, ROW_TABLE, ROW_TABLE),
+        in_specs=[SMEM, VMEM, VMEM],
+        out_specs=(VMEM,) * 4,
+        compiler_params=pltpu.CompilerParams(vmem_limit_bytes=16 * 2**20),
+        name="first_rows",
+    )(start, crop, sums)
+
+
+def second_rows_kernel(start_ref, sums, row_hi, row_lo, send_ref, keep_ref):
+    row_stage(start_ref[0], sums, row_hi, row_lo, send_ref, keep_ref)
+
+
+def second_rows_call(start, sums, row_hi, row_lo):
+    return pl.pallas_call(
+        second_rows_kernel,
         out_shape=(OCTET, OCTET),
         in_specs=[SMEM, VMEM, VMEM, VMEM],
         out_specs=(VMEM, VMEM),
         cost_estimate=pl.CostEstimate(flops=800_000_000, bytes_accessed=4_000_000, transcendentals=0),
         compiler_params=pltpu.CompilerParams(vmem_limit_bytes=16 * 2**20),
-        name="rows",
+        name="second_rows",
     )(start, sums, row_hi, row_lo)
 
 
@@ -226,7 +230,7 @@
     del after_ref
     scale = 1.0 / math.sqrt(NC)
     c = lax.broadcasted_iota(jnp.int32, (NC, CROP), 0)
-    q = crop_ref[1] + lax.broadcasted_iota(jnp.int32, (NC, CROP), 1)
+    q = crop_ref[0:1, 1:2] + lax.broadcasted_iota(jnp.int32, (NC, CROP), 1)
     cos, sin = cos_sin(((c * q) & (NC - 1)) * (TURN // NC))
     for lane, val in ((0, cos * scale), (128, sin * scale)):
         hi, lo = split(val)
@@ -239,8 +243,8 @@
     return pl.pallas_call(
         table_kernel,
         out_shape=(out, out),
-        in_specs=[SMEM, pl.BlockSpec(memory_space=pl.ANY)],
-        out_specs=(pl.BlockSpec(memory_space=pltpu.VMEM),) * 2,
+        in_specs=[VMEM, pl.BlockSpec(memory_space=pl.ANY)],
+        out_specs=(VMEM,) * 2,
         cost_estimate=pl.CostEstimate(flops=4_000_000, bytes_accessed=4_000_000, transcendentals=0),
         compiler_params=pltpu.CompilerParams(vmem_limit_bytes=8 * 2**20),
         name="table",
@@ -268,9 +272,11 @@
 
 def on_device(interferogram, sideband_start, crop_start):
     cores = [(0, 1), (1, 0)]
-    send0, keep0, later, *row_table = spectrum_call(sideband_start, crop_start, interferogram)
+    crop_start = crop_start.reshape(1, 2)
+    first, second = spectrum_call(sideband_start, interferogram)
+    send0, keep0, *row_table = first_rows_call(sideband_start, crop_start, first)
     got0 = lax.ppermute(send0, "core", cores)
-    send1, keep1 = row_call(sideband_start, later, *row_table)
+    send1, keep1 = second_rows_call(sideband_start, second, *row_table)
     got1 = lax.ppermute(send1, "core", cores)
     got1, table = lax.optimization_barrier((got1, table_call(crop_start, got0)))
     mine = assemble_call(keep0, got0, keep1, got1).reshape(64, 64, 128)

time: 58.5 us -> 57.5 us (0.983)
  local copies, waits for them, and re-layouts: 0.65 us -> 0.01 us
  Pallas kernels: 13.6 us -> 13 us
    unnamed x2, local copies, waits for them, and re-layouts: 0.65 us -> 0.01 us
    pallas_call x3 -> x4, Pallas kernels: 12 us -> 11.4 us  [the longest x1 7.96 us: spectrum_call(): pl.pallas_call(spectrum_kernel, out_shape=(jax.ShapeDtypeStruct((4, 1024,...]
where the time goes in v6:
time: 57.5 us; the launch traced here: 57.4 us
  blocking collectives  41.4 us (72%)
  Pallas kernels  13 us (23%)
  waiting for transfers between devices  1.51 us (3%)
  between operations  0.71 us (1%)
  starting transfers between devices  0.66 us (1%)
    all_to_all x1, blocking collectives, on_device(): lax.all_to_all(mine, ('half', 'col'), split_axis=0, concat_axis=0, tiled=...  41.4 us
    pallas_call x1, Pallas kernels, spectrum_call(): pl.pallas_call(spectrum_kernel, out_shape=(jax.ShapeDtypeStruct((4, 1024,...  7.96 us
    pallas_call x1, Pallas kernels, first_rows_call(): pl.pallas_call(first_rows_kernel, out_shape=(OCTET, OCTET, ROW_TABLE, ROW...  1.38 us
    pallas_call x1, Pallas kernels, focal_call(): pl.pallas_call(focal_kernel, out_shape=jax.ShapeDtypeStruct((2, 2, CROP,...  1.33 us
    pallas_call x1, Pallas kernels, second_rows_call(): pl.pallas_call(second_rows_kernel, out_shape=(OCTET, OCTET), in_specs=[SM...  1.27 us
  transfers between devices with their start and end apart: 2, of which 2 were waited for; matrix products, arithmetic and copies ran while one was open for 0% of the time, Pallas kernels for 4%

profile of v6, /device:TPU:0, one launch (start us, length us, event | category | flops | bytes accessed | tf_op | source)
XLA Modules:
  0.0 57.4 jit_solution(10793204070170899694)
XLA Ops:
  0.7 0.0 copy-start
  0.7 8.0 %spectrum.1 = (f32[4,1024,128]{2,1,0:T(8,128)S(1)}, f32[4,1024,128]{2,1,0:T(8,128)S(1)}) custom-call(s32[1]{0:T(128)S(6)} %copy.4.start_ref, f32[128,2,8,2048]{3,2,1,0:T(8,128)} %bitcast.16), custom_call_target="tpu_custom_call" | custom-call | tf_op jit(solution)/shard_map/spectrum/pallas_call | solution.py:155
  8.6 0.0 copy-done
  8.6 1.4 %first_rows.1 = (f32[2048,128]{1,0:T(8,128)S(1)}, f32[2048,128]{1,0:T(8,128)S(1)}, bf16[256,256]{1,0:T(8,128)(2,1)S(1)}, bf16[256,256]{1,0:T(8,128)(2,1)S(1)}) custom-call(s32[1]{0:T(128)S(6)} %copy.4.start_ref, s32[1,2]{1,0:T(1,128)S(1)} %bitcast.14, f32[4,1024,128]{2,1,0:T(8,128)S(1)} %get-tuple-element.19.sums), custom_call_target="tpu_custom_call" | custom-call | tf_op jit(solution)/shard_map/first_rows/pallas_call | solution.py:185
  10.0 0.1 collective-permute-start.1
  10.1 1.3 %second_rows.1 = (f32[2048,128]{1,0:T(8,128)S(1)}, f32[2048,128]{1,0:T(8,128)S(1)}) custom-call(s32[1]{0:T(128)S(6)} %copy.4.start_ref, f32[4,1024,128]{2,1,0:T(8,128)S(1)} %get-tuple-element.18.sums, bf16[256,256]{1,0:T(8,128)(2,1)S(1)} %get-tuple-element.20.row_hi, bf16[256,256]{1,0:T(8,128)(2,1)S(1)} %get-tuple-element.21.row_lo), custom_call_target="tpu_custom_call" | custom-call | flops 800000000 | bytes 4000000 | tf_op jit(solution)/shard_map/second_rows/pallas_call | solution.py:200
  11.4 0.6 collective-permute-start
  12.0 0.8 %collective-permute-done.1.after_ref = f32[2048,128]{1,0:T(8,128)S(1)} collective-permute-done((f32[2048,128]{1,0:T(8,128)S(1)}, f32[2048,128]{1,0:T(8,128)S(1)}, u32[]{:S(2)}, u32[]{:S(2)}) %collective-permute-start.1) | collective-permute-done | bytes 1048608 | tf_op jit(solution)/shard_map/ppermute | solution.py:278
  12.8 0.8 %table.1 = (bf16[512,256]{1,0:T(8,128)(2,1)S(1)}, bf16[512,256]{1,0:T(8,128)(2,1)S(1)}) custom-call(s32[1,2]{1,0:T(1,128)S(1)} %bitcast.15, f32[2048,128]{1,0:T(8,128)S(1)} %collective-permute-done.1.after_ref), custom_call_target="tpu_custom_call" | custom-call | flops 4000000 | bytes 4000000 | tf_op jit(solution)/shard_map/table/pallas_call | solution.py:243
  13.6 0.7 %collective-permute-done = f32[2048,128]{1,0:T(8,128)S(1)} collective-permute-done((f32[2048,128]{1,0:T(8,128)S(1)}, f32[2048,128]{1,0:T(8,128)S(1)}, u32[]{:S(2)}, u32[]{:S(2)}) %collective-permute-start) | collective-permute-done | bytes 1048608 | tf_op jit(solution)/shard_map/ppermute | solution.py:280
  14.3 0.3 assemble.1
  14.6 41.4 %all_to_all.5 = f32[64,64,128]{2,1,0:T(8,128)S(1)} all-to-all(f32[64,64,128]{2,1,0:T(8,128)S(1)} %bitcast.8), channel_id=1, replica_groups=mesh['half'=2,'core'=2,'col'=32] {'half','col'}, dimensions={0} | all-to-all | bytes 4194304 | tf_op jit(solution)/shard_map/all_to_all | solution.py:283
  56.0 1.3 %focal.1 = f32[2,2,128,128]{3,2,1,0:T(8,128)} custom-call(bf16[512,256]{1,0:T(8,128)(2,1)S(1)} %get-tuple-element.26.hi_ref, bf16[512,256]{1,0:T(8,128)(2,1)S(1)} %get-tuple-element.27.lo_ref, f32[64,4,16,128]{3,2,1,0:T(8,128)S(1)} %bitcast.9), custom_call_target="tpu_custom_call" | custom-call | tf_op jit(solution)/shard_map/focal/pallas_call | solution.py:263
Async XLA Ops:
  0.7 8.0 %copy-start = (s32[2]{0:T(128)S(1)}, s32[2]{0:T(128)}, u32[]{:S(2)}) copy-start(s32[2]{0:T(128)} %param.5) | copy-start | bytes 28
  10.0 2.7 %collective-permute-start.1 = (f32[2048,128]{1,0:T(8,128)S(1)}, f32[2048,128]{1,0:T(8,128)S(1)}, u32[]{:S(2)}, u32[]{:S(2)}) collective-permute-start(f32[2048,128]{1,0:T(8,128)S(1)} %get-tuple-element.23), channel_id=1, source_target_pairs={{0,32},{32,0},{1,33},{33,1},{2,34},{34,2},{3,35},{35,3},{4,36},{36... | collective-permute-start | bytes 3145736 | tf_op jit(solution)/shard_map/ppermute | solution.py:278
  11.4 2.9 %collective-permute-start = (f32[2048,128]{1,0:T(8,128)S(1)}, f32[2048,128]{1,0:T(8,128)S(1)}, u32[]{:S(2)}, u32[]{:S(2)}) collective-permute-start(f32[2048,128]{1,0:T(8,128)S(1)} %get-tuple-element.22), channel_id=1, source_target_pairs={{0,32},{32,0},{1,33},{33,1},{2,34},{34,2},{3,35},{35,3},{4,36},{36... | collective-permute-start | bytes 3145736 | tf_op jit(solution)/shard_map/ppermute | solution.py:280

commit v7 on v6

--- a/solution.py
+++ b/solution.py
@@ -44,7 +44,8 @@
 
 
 def dot3(a, b, dims):
-    return dot(a[0], b[0], dims) + (dot(a[0], b[1], dims) + dot(a[1], b[0], dims))
+    at = dims[0][0]
+    return dot(jnp.concatenate([a[0], a[0], a[1]], axis=at), jnp.concatenate([b[0], b[1], b[0]], axis=0), dims)
 
 
 NN_DIMS = ((1,), (0,))
@@ -174,10 +175,11 @@
     p = crop + lax.broadcasted_iota(jnp.int32, (128, CROP), 1)
     cos, sin = cos_sin(((r * p) & (NR - 1)) * (TURN // NR))
     cos, sin = cos * rscale, sin * rscale
-    for rows, cols, val in ((0, 0, cos), (0, 128, -sin), (128, 0, sin), (128, 128, cos)):
-        hi, lo = split(val)
-        row_hi[rows : rows + 128, cols : cols + 128] = hi
-        row_lo[rows : rows + 128, cols : cols + 128] = lo
+    for table, c, s in zip((row_hi, row_lo), split(cos), split(sin)):
+        table[0:128, 0:128] = c
+        table[0:128, 128:256] = -s
+        table[128:256, 0:128] = s
+        table[128:256, 128:256] = c
     row_stage(start_ref[0], sums, row_hi, row_lo, send_ref, keep_ref)
 
 

time: 57.5 us -> 57.5 us (level)
  no operation moved by 1% of the time
where the time goes in v7:
time: 57.5 us; the launch traced here: 57.4 us
  blocking collectives  41.4 us (72%)
  Pallas kernels  13 us (23%)
  waiting for transfers between devices  1.51 us (3%)
  between operations  0.71 us (1%)
  starting transfers between devices  0.66 us (1%)
    all_to_all x1, blocking collectives, on_device(): lax.all_to_all(mine, ('half', 'col'), split_axis=0, concat_axis=0, tiled=...  41.4 us
    pallas_call x1, Pallas kernels, spectrum_call(): pl.pallas_call(spectrum_kernel, out_shape=(jax.ShapeDtypeStruct((4, 1024,...  7.96 us
    pallas_call x1, Pallas kernels, first_rows_call(): pl.pallas_call(first_rows_kernel, out_shape=(OCTET, OCTET, ROW_TABLE, ROW...  1.38 us
    pallas_call x1, Pallas kernels, focal_call(): pl.pallas_call(focal_kernel, out_shape=jax.ShapeDtypeStruct((2, 2, CROP,...  1.34 us
    pallas_call x1, Pallas kernels, second_rows_call(): pl.pallas_call(second_rows_kernel, out_shape=(OCTET, OCTET), in_specs=[SM...  1.26 us
  transfers between devices with their start and end apart: 2, of which 2 were waited for; matrix products, arithmetic and copies ran while one was open for 0% of the time, Pallas kernels for 4%

profile of v7, /device:TPU:0, one launch (start us, length us, event | category | flops | bytes accessed | tf_op | source)
XLA Modules:
  0.0 57.4 jit_solution(10111888182497640349)
XLA Ops:
  0.7 0.0 copy-start
  0.7 8.0 %spectrum.1 = (f32[4,1024,128]{2,1,0:T(8,128)S(1)}, f32[4,1024,128]{2,1,0:T(8,128)S(1)}) custom-call(s32[1]{0:T(128)S(6)} %copy.4.start_ref, f32[128,2,8,2048]{3,2,1,0:T(8,128)} %bitcast.16), custom_call_target="tpu_custom_call" | custom-call | tf_op jit(solution)/shard_map/spectrum/pallas_call | solution.py:156
  8.6 0.0 copy-done
  8.6 1.4 %first_rows.1 = (f32[2048,128]{1,0:T(8,128)S(1)}, f32[2048,128]{1,0:T(8,128)S(1)}, bf16[256,256]{1,0:T(8,128)(2,1)S(1)}, bf16[256,256]{1,0:T(8,128)(2,1)S(1)}) custom-call(s32[1]{0:T(128)S(6)} %copy.4.start_ref, s32[1,2]{1,0:T(1,128)S(1)} %bitcast.14, f32[4,1024,128]{2,1,0:T(8,128)S(1)} %get-tuple-element.19.sums), custom_call_target="tpu_custom_call" | custom-call | tf_op jit(solution)/shard_map/first_rows/pallas_call | solution.py:187
  10.0 0.1 collective-permute-start.1
  10.1 1.3 %second_rows.1 = (f32[2048,128]{1,0:T(8,128)S(1)}, f32[2048,128]{1,0:T(8,128)S(1)}) custom-call(s32[1]{0:T(128)S(6)} %copy.4.start_ref, f32[4,1024,128]{2,1,0:T(8,128)S(1)} %get-tuple-element.18.sums, bf16[256,256]{1,0:T(8,128)(2,1)S(1)} %get-tuple-element.20.row_hi, bf16[256,256]{1,0:T(8,128)(2,1)S(1)} %get-tuple-element.21.row_lo), custom_call_target="tpu_custom_call" | custom-call | flops 800000000 | bytes 4000000 | tf_op jit(solution)/shard_map/second_rows/pallas_call | solution.py:202
  11.4 0.6 collective-permute-start
  12.0 0.8 %collective-permute-done.1.after_ref = f32[2048,128]{1,0:T(8,128)S(1)} collective-permute-done((f32[2048,128]{1,0:T(8,128)S(1)}, f32[2048,128]{1,0:T(8,128)S(1)}, u32[]{:S(2)}, u32[]{:S(2)}) %collective-permute-start.1) | collective-permute-done | bytes 1048608 | tf_op jit(solution)/shard_map/ppermute | solution.py:280
  12.8 0.8 %table.1 = (bf16[512,256]{1,0:T(8,128)(2,1)S(1)}, bf16[512,256]{1,0:T(8,128)(2,1)S(1)}) custom-call(s32[1,2]{1,0:T(1,128)S(1)} %bitcast.15, f32[2048,128]{1,0:T(8,128)S(1)} %collective-permute-done.1.after_ref), custom_call_target="tpu_custom_call" | custom-call | flops 4000000 | bytes 4000000 | tf_op jit(solution)/shard_map/table/pallas_call | solution.py:245
  13.6 0.7 %collective-permute-done = f32[2048,128]{1,0:T(8,128)S(1)} collective-permute-done((f32[2048,128]{1,0:T(8,128)S(1)}, f32[2048,128]{1,0:T(8,128)S(1)}, u32[]{:S(2)}, u32[]{:S(2)}) %collective-permute-start) | collective-permute-done | bytes 1048608 | tf_op jit(solution)/shard_map/ppermute | solution.py:282
  14.3 0.3 assemble.1
  14.6 41.4 %all_to_all.5 = f32[64,64,128]{2,1,0:T(8,128)S(1)} all-to-all(f32[64,64,128]{2,1,0:T(8,128)S(1)} %bitcast.8), channel_id=1, replica_groups=mesh['half'=2,'core'=2,'col'=32] {'half','col'}, dimensions={0} | all-to-all | bytes 4194304 | tf_op jit(solution)/shard_map/all_to_all | solution.py:285
  56.0 1.3 %focal.1 = f32[2,2,128,128]{3,2,1,0:T(8,128)} custom-call(bf16[512,256]{1,0:T(8,128)(2,1)S(1)} %get-tuple-element.26.hi_ref, bf16[512,256]{1,0:T(8,128)(2,1)S(1)} %get-tuple-element.27.lo_ref, f32[64,4,16,128]{3,2,1,0:T(8,128)S(1)} %bitcast.9), custom_call_target="tpu_custom_call" | custom-call | tf_op jit(solution)/shard_map/focal/pallas_call | solution.py:265
Async XLA Ops:
  0.7 8.0 %copy-start = (s32[2]{0:T(128)S(1)}, s32[2]{0:T(128)}, u32[]{:S(2)}) copy-start(s32[2]{0:T(128)} %param.5) | copy-start | bytes 28
  10.0 2.7 %collective-permute-start.1 = (f32[2048,128]{1,0:T(8,128)S(1)}, f32[2048,128]{1,0:T(8,128)S(1)}, u32[]{:S(2)}, u32[]{:S(2)}) collective-permute-start(f32[2048,128]{1,0:T(8,128)S(1)} %get-tuple-element.23), channel_id=1, source_target_pairs={{0,32},{32,0},{1,33},{33,1},{2,34},{34,2},{3,35},{35,3},{4,36},{36... | collective-permute-start | bytes 3145736 | tf_op jit(solution)/shard_map/ppermute | solution.py:280
  11.4 2.9 %collective-permute-start = (f32[2048,128]{1,0:T(8,128)S(1)}, f32[2048,128]{1,0:T(8,128)S(1)}, u32[]{:S(2)}, u32[]{:S(2)}) collective-permute-start(f32[2048,128]{1,0:T(8,128)S(1)} %get-tuple-element.22), channel_id=1, source_target_pairs={{0,32},{32,0},{1,33},{33,1},{2,34},{34,2},{3,35},{35,3},{4,36},{36... | collective-permute-start | bytes 3145736 | tf_op jit(solution)/shard_map/ppermute | solution.py:282
